TPU v7x, 32 devices: a whole 2x2x4 slice. The times are simulated.
32 devices in a mesh: groups: 2 (over y), streams: 8 (over z, x), segment: 2 (over core).
Axes of the slice: x: 2, y: 2, z: 4, core: 2. Of those that a mesh axis runs over, the one named last changes fastest.
Arguments:
- latent: bfloat16 [4096, 1024], P(('groups', 'streams'), 'segment'), parts along dimension 0, may hold values from -6 to 6
- conv_weight: bfloat16 [1024, 16, 512], P('streams', None, 'segment'), may hold values from -0.1875 to 0.1875
- conv_bias: float32 [512], P('segment'), may hold values from -3 to 3
- tail_cache: bfloat16 [128, 8, 512], P(('groups', 'streams'), None, 'segment'), parts along dimension 0, may hold values from -6 to 6
- input_cache: bfloat16 [128, 2, 512], P(('groups', 'streams'), None, 'segment'), parts along dimension 0, may hold values from -0.8984375 to 2
- resume_slot: int32 [128], P(('groups', 'streams')), parts along dimension 0, may hold values from -1 to 255, as said below
- res_weight: bfloat16 [3, 512, 256], P(None, 'segment'), may hold values from -0.15625 to 0.15625
- res_bias: float32 [256], replicated, may hold values from -3 to 3
- skip_weight: bfloat16 [256, 512], P(None, 'segment'), may hold values from -0.375 to 0.375
- skip_bias: float32 [512], P('segment'), may hold values from -3 to 3
Outputs:
- decoded: bfloat16 [4096, 8, 512], P(('groups', 'streams'), None, 'segment'), parts along dimension 0
- new_tail: bfloat16 [4096, 8, 512], P(('groups', 'streams'), None, 'segment'), parts along dimension 0
There are 2 independent parts, one for each index of `groups`. A program takes and returns all parts, laid end to end along the dimension named above; an argument that names none is the same for every part. Nothing has to cross between parts.
Inputs may be any that keep to these rules, and one draw needn't show every extreme that they name: `resume_slot`: slot k of an owner device's store serves decoder device k // 1 of the same index range; an entry is -1 (slot unused) or the position, among that decoder device's 256 rows in decoder order, of the session that resumes from it. No decoder row is named by two slots. In every draw there is one decoder device all of whose reserved slots are in use (none is -1).
All inputs are finite; a program needn't handle non-finite values.
Results may differ from a plain program's by a relative error of at most 0.0042.
Values may be sent and summed in bfloat16 or wider, within the bound.
No kernel may reach another device: no remote copies, remote signals or barrier semaphores. Data moves between devices by JAX's collectives and lax.ppermute only.
A program may use at most 64 MiB of HBM per device.

v0:
```python
import functools

import jax
import jax.numpy as jnp
from jax import lax
from jax.experimental import pallas as pl
from jax.experimental.pallas import tpu as pltpu
from jax.sharding import PartitionSpec as P

VMEM_LIMIT = 48 * 1024 * 1024
F32 = jnp.float32
BF16 = jnp.bfloat16


def apply_elu(values):
    return jnp.where(values > 0, values, jnp.exp(jnp.minimum(values, 0.0)) - 1.0)


def ring_order(count):
    return [2 * p if p < count // 2 else 2 * (count - 1 - p) + 1 for p in range(count)]


def ring_place(stream, count):
    return jnp.where(stream % 2 == 0, stream // 2, count - 1 - stream // 2)


def ring_stream(place, count):
    return jnp.where(place < count // 2, 2 * place, 2 * (count - 1 - place) + 1)


def spread_kernel(count, steps, *refs):
    blocks = refs[: len(steps)]
    sides, (home_ref, away_ref) = refs[len(steps) : len(steps) + 4], refs[len(steps) + 4 : -3]
    kernel_rows, inputs, sems = refs[-3:]
    rows = blocks[0].shape[-2]
    place = ring_place(lax.axis_index("streams"), count)
    copies = []
    for step, block in zip(steps, blocks):
        if step is None:
            pieces = [
                (block.at[stream], kernel_rows.at[:, pl.ds(stream * rows, rows), :])
                for stream in range(count)
            ]
        else:
            stream = ring_stream(lax.rem(place + step + count, count), count)
            pieces = [
                (block, kernel_rows.at[:, pl.ds(pl.multiple_of(stream * rows, rows), rows), :])
            ]
        for source, target in pieces:
            copy = pltpu.make_async_copy(source, target, sems.at[len(copies)])
            copy.start()
            copies.append(copy)
    half = sides[0].shape[1]
    mine = lax.axis_index("segment")
    for index, side in enumerate(sides):
        column = mine if index % 2 == 0 else 1 - mine
        inputs[index // 2, :, pl.ds(pl.multiple_of(column * half, half), half)] = side[...]
    for copy in copies:
        copy.wait()

    @pl.loop(0, kernel_rows.shape[0])
    def _(tap):
        weights = kernel_rows[tap]
        home_ref[tap] = jnp.dot(inputs[0], weights, preferred_element_type=F32).astype(
            home_ref.dtype
        )
        away_ref[tap] = jnp.dot(inputs[1], weights, preferred_element_type=F32).astype(
            away_ref.dtype
        )


def spread_taps(sides, blocks, steps, count, home_type):
    taps, _, width = blocks[0].shape[-3:]
    sessions, depth = sides[0].shape[0], 2 * sides[0].shape[1]
    vmem = pl.BlockSpec(memory_space=pltpu.VMEM)
    return pl.pallas_call(
        functools.partial(spread_kernel, count, steps),
        out_shape=(
            jax.ShapeDtypeStruct((taps, sessions, width), home_type),
            jax.ShapeDtypeStruct((taps, sessions, width), BF16),
        ),
        in_specs=[pl.BlockSpec(memory_space=pl.ANY)] * len(blocks) + [vmem] * 4,
        out_specs=(vmem, vmem),
        scratch_shapes=[
            pltpu.VMEM((taps, depth, width), BF16),
            pltpu.VMEM((2, sessions, depth), BF16),
            pltpu.SemaphoreType.DMA((count,)),
        ],
        compiler_params=pltpu.CompilerParams(vmem_limit_bytes=VMEM_LIMIT),
        cost_estimate=pl.CostEstimate(
            flops=4 * taps * sessions * depth * width,
            bytes_accessed=2 * taps * depth * width + 4 * sessions * depth + 6 * taps * sessions * width,
            transcendentals=0,
        ),
    )(*blocks, *sides)


def excite_kernel(group_ref, own_ref, other_ref, prev_ref, bias_ref, up_ref, window_ref):
    taps = own_ref.shape[0]
    bias = bias_ref[...]
    group = group_ref[0]
    history = prev_ref.shape[0] - 2 * taps
    for step in range(history):
        window_ref[step] = prev_ref[2 * taps + step]
    for half in range(2):
        for tap in range(taps):
            value = jnp.where(group == half, own_ref[tap], other_ref[tap].astype(F32))
            step = half * taps + tap
            up = value + prev_ref[step].astype(F32) + bias
            up_ref[step] = up
            window_ref[history + step] = apply_elu(up).astype(BF16)


def excite(group, own, other, prev, bias):
    taps, sessions, width = own.shape
    vmem = pl.BlockSpec(memory_space=pltpu.VMEM)
    return pl.pallas_call(
        excite_kernel,
        out_shape=(
            jax.ShapeDtypeStruct((2 * taps, sessions, width), F32),
            jax.ShapeDtypeStruct((prev.shape[0], sessions, width), BF16),
        ),
        in_specs=[pl.BlockSpec(memory_space=pltpu.SMEM), vmem, vmem, vmem, vmem],
        out_specs=(vmem, vmem),
        compiler_params=pltpu.CompilerParams(vmem_limit_bytes=VMEM_LIMIT),
        cost_estimate=pl.CostEstimate(
            flops=20 * taps * sessions * width,
            bytes_accessed=40 * taps * sessions * width,
            transcendentals=2 * taps * sessions * width,
        ),
    )(group, own, other, prev, bias)


def residual_kernel(
    up_ref, mine_ref, theirs_ref, res_mine_ref, res_theirs_ref, res_bias_ref, skip_ref, skip_bias_ref, out_ref
):
    @pl.loop(0, up_ref.shape[0])
    def _(step):
        branch = jnp.zeros(up_ref.shape[1:2] + res_mine_ref.shape[2:], F32)
        for offset in range(res_mine_ref.shape[0]):
            branch += jnp.dot(
                mine_ref[step + offset], res_mine_ref[offset], preferred_element_type=F32
            )
            branch += jnp.dot(
                theirs_ref[step + offset], res_theirs_ref[offset], preferred_element_type=F32
            )
        hidden = apply_elu(branch + res_bias_ref[...]).astype(BF16)
        projected = jnp.dot(hidden, skip_ref[...], preferred_element_type=F32)
        out_ref[step] = (up_ref[step] + projected + skip_bias_ref[...]).astype(BF16)


def residual(up, mine, theirs, res_mine, res_theirs, res_bias, skip_weight, skip_bias):
    vmem = pl.BlockSpec(memory_space=pltpu.VMEM)
    return pl.pallas_call(
        residual_kernel,
        out_shape=jax.ShapeDtypeStruct(up.shape, BF16),
        in_specs=[vmem] * 8,
        out_specs=vmem,
        compiler_params=pltpu.CompilerParams(vmem_limit_bytes=VMEM_LIMIT),
        cost_estimate=pl.CostEstimate(
            flops=2 * up.size * (2 * res_mine.shape[0] + 1) * res_mine.shape[2],
            bytes_accessed=12 * up.size,
            transcendentals=up.size,
        ),
    )(up, mine, theirs, res_mine, res_theirs, res_bias, skip_weight, skip_bias)


def swap(value, axis):
    return lax.ppermute(value, axis, [(0, 1), (1, 0)])


def local(
    count,
    latent,
    conv_weight,
    conv_bias,
    tail_cache,
    input_cache,
    resume_slot,
    res_weight,
    res_bias,
    skip_weight,
    skip_bias,
):
    group = lax.axis_index("groups")
    rows, tap_count, width = conv_weight.shape
    sessions = latent.shape[0]
    taps = tap_count // 4

    halves = []
    for first in (0, tap_count // 2):
        part = lax.dynamic_slice_in_dim(conv_weight, first + group * taps, taps, axis=1)
        halves.append(part.transpose(1, 0, 2))

    portion = sessions // count
    cap = tail_cache.shape[0] // count
    half_taps, history = tail_cache.shape[1], input_cache.shape[1]
    slot_step = jnp.broadcast_to(
        resume_slot.astype(BF16)[:, None, None], (count * cap, 1, width)
    )
    filler = jnp.zeros((count * cap, half_taps - history - 1, width), BF16)
    beside = jnp.concatenate([input_cache, slot_step, filler], axis=1)
    stored = jnp.concatenate([tail_cache, beside], axis=2).reshape(count, cap * half_taps, 2 * width)
    parcel = jnp.concatenate([latent.reshape(count, portion, 2 * width), stored], axis=1)
    parcel = lax.all_to_all(parcel, "streams", split_axis=0, concat_axis=0, tiled=True)
    handed = parcel[:, :portion].reshape(sessions, 2 * width)
    stored = parcel[:, portion:].reshape(count * cap, half_taps, 2 * width)

    near_half = apply_elu(handed.astype(F32)).astype(BF16)
    far_half = swap(near_half, "groups")
    sides = (near_half, swap(near_half, "segment"), far_half, swap(far_half, "segment"))

    slots = stored[:, history, width:].astype(jnp.int32)[:, :1]
    one_hot = (slots == jnp.arange(sessions, dtype=jnp.int32)[None, :]).astype(BF16)
    packed = jnp.concatenate([stored[:, :, :width], stored[:, :history, width:]], axis=1)
    prev = jnp.einsum("js,jkc->ksc", one_hot, packed, preferred_element_type=F32).astype(BF16)

    res_theirs = swap(res_weight, "segment")

    def gather_all(own):
        return [lax.all_gather(own, "streams", axis=0)], [None]

    def gather_ring(own):
        order = ring_order(count)
        onward = [(order[p], order[(p + 1) % count]) for p in range(count)]
        back = [(b, a) for a, b in onward]
        blocks, steps = [own], [0]
        item = ahead = own
        for r in range(1, count // 2 + 1):
            item = lax.ppermute(item, "streams", onward)
            blocks.append(item)
            steps.append(-r)
            if 2 * r < count:
                ahead = lax.ppermute(ahead, "streams", back)
                blocks.append(ahead)
                steps.append(r)
        return blocks, steps

    use_ring = rows % 128 == 0 and count % 2 == 0
    gathered = [(gather_ring if use_ring else gather_all)(halves[0]), gather_all(halves[1])]

    own_up, away_up = spread_taps(sides, *gathered[0], count, F32)
    other_up = swap(away_up, "groups")
    own_tail, away_tail = spread_taps(sides, *gathered[1], count, BF16)
    other_tail = swap(away_tail, "groups")

    up, mine = excite(group[None].astype(jnp.int32), own_up, other_up, prev, conv_bias[None])
    theirs = swap(mine, "segment")
    decoded = residual(
        up, mine, theirs, res_weight, res_theirs, res_bias[None], skip_weight, skip_bias[None]
    )
    decoded = decoded.transpose(1, 0, 2)
    decoded, other_tail = lax.optimization_barrier((decoded, other_tail))
    first = jnp.where(group == 0, own_tail, other_tail)
    second = jnp.where(group == 0, other_tail, own_tail)
    new_tail = jnp.concatenate([first, second], axis=0).transpose(1, 0, 2)
    return decoded, new_tail


def solution(mesh):
    placed = (
        P(("groups", "streams"), "segment"),
        P("streams", None, "segment"),
        P("segment"),
        P(("groups", "streams"), None, "segment"),
        P(("groups", "streams"), None, "segment"),
        P(("groups", "streams")),
        P(None, "segment", None),
        P(),
        P(None, "segment"),
        P("segment"),
    )
    return jax.shard_map(
        functools.partial(local, mesh.shape["streams"]),
        mesh=mesh,
        in_specs=placed,
        out_specs=(
            P(("groups", "streams"), None, "segment"),
            P(("groups", "streams"), None, "segment"),
        ),
        check_vma=False,
    )
```

profile of v0, /device:TPU:0, one launch (start us, length us, event | category | flops | bytes accessed | tf_op | source)
XLA Modules:
  0.0 123.5 jit_solution(6340715579982913769)
XLA Ops:
  7.2 0.0 all-gather.3.cloned.1.call-start
  7.3 1.5 %constant_dynamic-slice_fusion = (bf16[128,4,256]{2,1,0:T(4,128)(2,1)S(1)}, bf16[128,4,256]{2,1,0:T(4,128)(2,1)S(1)}) fusion(bf16[128,16,256]{2,1,0:T(8,128)(2,1)} %param.11, s32[]{:T(128)S(6)} %select_n.24, s32[]{:T(128)S(6)} %select_n.22), kind=kLoop, calls=%fused_computation.21 | loop fusion | bytes 1048584 | tf_op jit(solution)/shard_map/dynamic_slice | solution.py:192
  8.8 0.7 copy.53
  9.5 0.0 all-gather.3.cloned.1.call-update
  9.6 0.1 broadcast_in_dim.23
  9.7 0.8 maximum_maximum_fusion
  10.5 7.3 %all-to-all-start = ((bf16[8,40,512]{2,1,0:T(8,128)(2,1)}), bf16[8,40,512]{2,1,0:T(8,128)(2,1)S(1)}, u32[]{:S(2)}, u32[]{:S(2)}) async-start(bf16[8,40,512]{2,1,0:T(8,128)(2,1)} %maximum_maximum_fusion), calls=%async_computation | async-start | bytes 655360 | tf_op jit(solution)/shard_map/all_to_all | solution.py:205
  17.8 2.1 %collective-permute-start = (bf16[4,128,256]{2,1,0:T(8,128)(2,1)S(1)}, bf16[4,128,256]{2,1,0:T(8,128)(2,1)S(1)}, u32[]{:S(2)}, u32[]{:S(2)}) collective-permute-start(bf16[4,128,256]{2,1,0:T(8,128)(2,1)S(1)} %bitcast.27), channel_id=1, source_target_pairs={{0,4},{4,8},{8,12},{12,14},{14,10},{10,6},{6,2},{2,0},{1,5},{5,9},... | collective-permute-start | bytes 786440 | tf_op jit(solution)/shard_map/ppermute | solution.py:230
  19.8 0.1 collective-permute-start.1
  19.9 16.5 %collective-permute-done.refs_1_ = bf16[4,128,256]{2,1,0:T(8,128)(2,1)S(1)} collective-permute-done((bf16[4,128,256]{2,1,0:T(8,128)(2,1)S(1)}, bf16[4,128,256]{2,1,0:T(8,128)(2,1)S(1)}, u32[]{:S(2)}, u32[]{:S(2)}) %collective-permute-start) | collective-permute-done | bytes 262176 | tf_op jit(solution)/shard_map/ppermute | solution.py:230
  36.4 4.0 %collective-permute-start.2 = (bf16[4,128,256]{2,1,0:T(8,128)(2,1)S(1)}, bf16[4,128,256]{2,1,0:T(8,128)(2,1)S(1)}, u32[]{:S(2)}, u32[]{:S(2)}) collective-permute-start(bf16[4,128,256]{2,1,0:T(8,128)(2,1)S(1)} %collective-permute-done.refs_1_), channel_id=1, source_target_pairs={{0,4},{4,8},{8,12},{12,14},{14,10},{10,6},{6,2},{2,0},{1,5},{5,9},... | collective-permute-start | bytes 786440 | tf_op jit(solution)/shard_map/ppermute | solution.py:230
  40.4 0.0 collective-permute-done.1.refs_2_
  40.4 0.0 collective-permute-start.3
  40.4 5.8 %collective-permute-done.2.refs_3_ = bf16[4,128,256]{2,1,0:T(8,128)(2,1)S(1)} collective-permute-done((bf16[4,128,256]{2,1,0:T(8,128)(2,1)S(1)}, bf16[4,128,256]{2,1,0:T(8,128)(2,1)S(1)}, u32[]{:S(2)}, u32[]{:S(2)}) %collective-permute-start.2) | collective-permute-done | bytes 262176 | tf_op jit(solution)/shard_map/ppermute | solution.py:230
  46.2 7.3 %collective-permute-start.4 = (bf16[4,128,256]{2,1,0:T(8,128)(2,1)S(1)}, bf16[4,128,256]{2,1,0:T(8,128)(2,1)S(1)}, u32[]{:S(2)}, u32[]{:S(2)}) collective-permute-start(bf16[4,128,256]{2,1,0:T(8,128)(2,1)S(1)} %collective-permute-done.2.refs_3_), channel_id=1, source_target_pairs={{0,4},{4,8},{8,12},{12,14},{14,10},{10,6},{6,2},{2,0},{1,5},{5,9},... | collective-permute-start | bytes 786440 | tf_op jit(solution)/shard_map/ppermute | solution.py:230
  53.5 0.1 fusion.3.refs_8_.refs_1_
  53.6 1.2 collective-permute-start.8
  54.8 0.0 collective-permute-done.3.refs_4_
  54.8 0.0 collective-permute-start.5
  54.8 0.0 collective-permute-start.7
  54.8 8.3 %collective-permute-done.4.refs_5_ = bf16[4,128,256]{2,1,0:T(8,128)(2,1)S(1)} collective-permute-done((bf16[4,128,256]{2,1,0:T(8,128)(2,1)S(1)}, bf16[4,128,256]{2,1,0:T(8,128)(2,1)S(1)}, u32[]{:S(2)}, u32[]{:S(2)}) %collective-permute-start.4) | collective-permute-done | bytes 262176 | tf_op jit(solution)/shard_map/ppermute | solution.py:230
  63.1 6.7 %collective-permute-start.6 = (bf16[4,128,256]{2,1,0:T(8,128)(2,1)S(1)}, bf16[4,128,256]{2,1,0:T(8,128)(2,1)S(1)}, u32[]{:S(2)}, u32[]{:S(2)}) collective-permute-start(bf16[4,128,256]{2,1,0:T(8,128)(2,1)S(1)} %collective-permute-done.4.refs_5_), channel_id=1, source_target_pairs={{0,4},{4,8},{8,12},{12,14},{14,10},{10,6},{6,2},{2,0},{1,5},{5,9},... | collective-permute-start | bytes 786440 | tf_op jit(solution)/shard_map/ppermute | solution.py:230
  69.8 0.0 collective-permute-done.8.refs_10_.refs_3_
  69.8 0.0 collective-permute-start.9
  69.8 1.4 %collective-permute-done.5.refs_6_ = bf16[4,128,256]{2,1,0:T(8,128)(2,1)S(1)} collective-permute-done((bf16[4,128,256]{2,1,0:T(8,128)(2,1)S(1)}, bf16[4,128,256]{2,1,0:T(8,128)(2,1)S(1)}, u32[]{:S(2)}, u32[]{:S(2)}) %collective-permute-start.5) | collective-permute-done | bytes 262176 | tf_op jit(solution)/shard_map/ppermute | solution.py:234
  71.2 0.0 collective-permute-done.7.refs_9_.refs_2_
  71.2 5.9 %collective-permute-done.6.refs_7_ = bf16[4,128,256]{2,1,0:T(8,128)(2,1)S(1)} collective-permute-done((bf16[4,128,256]{2,1,0:T(8,128)(2,1)S(1)}, bf16[4,128,256]{2,1,0:T(8,128)(2,1)S(1)}, u32[]{:S(2)}, u32[]{:S(2)}) %collective-permute-start.6) | collective-permute-done | bytes 262176 | tf_op jit(solution)/shard_map/ppermute | solution.py:230
  77.1 0.0 collective-permute-done.9.refs_11_.refs_4_
  77.1 2.1 %shard_map.113 = (f32[4,256,256]{2,1,0:T(8,128)S(1)}, bf16[4,256,256]{2,1,0:T(8,128)(2,1)S(1)}) custom-call(bf16[4,128,256]{2,1,0:T(8,128)(2,1)S(1)} %bitcast.29, bf16[4,128,256]{2,1,0:T(8,128)(2,1)S(1)} %collective-permute-done.refs_1_, bf16[4,128,256]{2,1,0:T(8,128)(2,1)S(1)} %collective-permute-done.1.refs_2_, ...), custom_call_target="tpu_custom_call" | custom-call | flops 1073741824 | bytes 4718592 | tf_op jit(solution)/shard_map/pallas_call | solution.py:76
  79.2 0.0 copy-start
  79.2 1.6 %collective-permute-start.10 = (bf16[4,256,256]{2,1,0:T(8,128)(2,1)S(1)}, bf16[4,256,256]{2,1,0:T(8,128)(2,1)S(1)}, u32[]{:S(2)}, u32[]{:S(2)}) collective-permute-start(bf16[4,256,256]{2,1,0:T(8,128)(2,1)S(1)} %get-tuple-element.11), channel_id=1, source_target_pairs={{0,16},{16,0},{1,17},{17,1},{2,18},{18,2},{3,19},{19,3},{4,20},{20... | collective-permute-start | bytes 1572872 | tf_op jit(solution)/shard_map/ppermute | solution.py:169
  80.9 0.1 convert_reduce_fusion
  81.0 0.6 fusion.prev_ref
  81.7 6.8 %collective-permute-done.10.other_ref = bf16[4,256,256]{2,1,0:T(8,128)(2,1)S(1)} collective-permute-done((bf16[4,256,256]{2,1,0:T(8,128)(2,1)S(1)}, bf16[4,256,256]{2,1,0:T(8,128)(2,1)S(1)}, u32[]{:S(2)}, u32[]{:S(2)}) %collective-permute-start.10) | collective-permute-done | bytes 524320 | tf_op jit(solution)/shard_map/ppermute | solution.py:169
  88.5 1.8 %shard_map.114 = (f32[8,256,256]{2,1,0:T(8,128)}, bf16[10,256,256]{2,1,0:T(8,128)(2,1)S(1)}) custom-call(s32[1]{0:T(128)} %bitcast.group_ref, f32[4,256,256]{2,1,0:T(8,128)S(1)} %get-tuple-element.10.own_ref, bf16[4,256,256]{2,1,0:T(8,128)(2,1)S(1)} %collective-permute-done.10.other_ref, bf16[10,256,256]{2,1,0:T(8,128)(2,1)S(1)} %fusion.prev_ref, ...), custom_call_target="tpu_custom_call" | custom-call | flops 5242880 | bytes 10485760 | tf_op jit(solution)/shard_map/pallas_call | solution.py:117
  90.3 0.5 collective-permute-start.12
  90.8 1.6 %copy-done.1 = bf16[32,128,256]{2,1,0:T(8,128)(2,1)S(1)} copy-done((bf16[32,128,256]{2,1,0:T(8,128)(2,1)S(1)}, bf16[32,128,256]{2,1,0:T(8,128)(2,1)}, u32[]{:S(2)}) %copy-start.1) | copy-done | bytes 2097176
  92.4 0.9 copy-done.3
  93.3 0.9 copy-done.5
  94.3 0.9 copy-done.7
  95.2 2.9 %shard_map.116 = (bf16[4,256,256]{2,1,0:T(8,128)(2,1)S(1)}, bf16[4,256,256]{2,1,0:T(8,128)(2,1)}) custom-call(bf16[8,4,128,256]{3,2,1,0:T(8,128)(2,1)S(1)} %bitcast.31, bf16[256,512]{1,0:T(8,128)(2,1)S(1)} %fusion.3.refs_8_.refs_1_, bf16[256,512]{1,0:T(8,128)(2,1)S(1)} %copy-done.5, bf16[256,512]{1,0:T(8,128)(2,1)S(1)} %copy-done.3, ...), custom_call_target="tpu_custom_call" | custom-call | flops 1073741824 | bytes 4718592 | tf_op jit(solution)/shard_map/pallas_call | solution.py:76
  98.1 1.6 %collective-permute-start.13 = (bf16[4,256,256]{2,1,0:T(8,128)(2,1)}, bf16[4,256,256]{2,1,0:T(8,128)(2,1)}, u32[]{:S(2)}, u32[]{:S(2)}) collective-permute-start(bf16[4,256,256]{2,1,0:T(8,128)(2,1)} %get-tuple-element.14), channel_id=1, source_target_pairs={{0,16},{16,0},{1,17},{17,1},{2,18},{18,2},{3,19},{19,3},{4,20},{20... | collective-permute-start | bytes 1572872 | tf_op jit(solution)/shard_map/ppermute | solution.py:169
  99.7 6.1 %shard_map.115 = bf16[8,256,256]{2,1,0:T(8,128)(2,1)S(1)} custom-call(f32[8,256,256]{2,1,0:T(8,128)} %get-tuple-element.12.up_ref, bf16[10,256,256]{2,1,0:T(8,128)(2,1)S(1)} %get-tuple-element.13.mine_ref, bf16[10,256,256]{2,1,0:T(8,128)(2,1)S(1)} %collective-permute-done.11.theirs_ref, bf16[3,256,256]{2,1,0:T(8,128)(2,1)} %res_mine_ref.1, ...), custom_call_target="tpu_custom_call" | custom-call | flops 1879048192 | bytes 6291456 | tf_op jit(solution)/shard_map/pallas_call | solution.py:154
  105.8 6.5 %collective-permute-done.13 = bf16[4,256,256]{2,1,0:T(8,128)(2,1)} collective-permute-done((bf16[4,256,256]{2,1,0:T(8,128)(2,1)}, bf16[4,256,256]{2,1,0:T(8,128)(2,1)}, u32[]{:S(2)}, u32[]{:S(2)}) %collective-permute-start.13) | collective-permute-done | bytes 524320 | tf_op jit(solution)/shard_map/ppermute | solution.py:169
  112.3 1.1 broadcast_select_fusion.1
  113.4 0.1 maximum_bitcast_fusion
  113.5 1.6 %copy.43 = bf16[256,8,256]{2,1,0:T(8,128)(2,1)} copy(bf16[256,8,256]{2,0,1:T(8,128)(2,1)S(1)} %maximum_bitcast_fusion) | data formatting | bytes 2097152
  115.1 1.6 %copy.42 = bf16[256,8,256]{2,1,0:T(8,128)(2,1)} copy(bf16[256,8,256]{2,0,1:T(8,128)(2,1)S(1)} %bitcast.26) | data formatting | bytes 2097152
  (41 shorter events, 0.2 us)
Async XLA Ops:
  7.2 2.4 %copy-start.14 = (s32[8]{0:T(128)S(1)}, s32[8]{0:T(128)}, u32[]{:S(2)}) copy-start(s32[8]{0:T(128)} %param.15) | copy-start | bytes 100
  7.2 2.5 %copy-start.11 = (bf16[256,512]{1,0:T(8,128)(2,1)S(1)}, bf16[256,512]{1,0:T(8,128)(2,1)}, u32[]{:S(2)}) copy-start(bf16[256,512]{1,0:T(8,128)(2,1)} %param.10) | copy-start | bytes 786436
  7.2 2.5 %copy-start.12 = (bf16[8,8,256]{2,1,0:T(8,128)(2,1)S(1)}, bf16[8,8,256]{2,1,0:T(8,128)(2,1)}, u32[]{:S(2)}) copy-start(bf16[8,8,256]{2,1,0:T(8,128)(2,1)} %param.13) | copy-start | bytes 98308
  7.2 2.5 %copy-start.13 = (bf16[8,2,256]{2,1,0:T(2,128)(2,1)S(1)}, bf16[8,2,256]{2,1,0:T(2,128)(2,1)}, u32[]{:S(2)}) copy-start(bf16[8,2,256]{2,1,0:T(2,128)(2,1)} %param.14) | copy-start | bytes 24580
  7.2 83.6 %all-gather.3.cloned.1.call-start = ((), (), s32[]{:S(2)}) async-start(), calls=%async_computation.1 | async-start | bytes 2359296 | tf_op jit(solution)/shard_map/all_gather | solution.py:221
  10.5 43.0 %all-to-all-start = ((bf16[8,40,512]{2,1,0:T(8,128)(2,1)}), bf16[8,40,512]{2,1,0:T(8,128)(2,1)S(1)}, u32[]{:S(2)}, u32[]{:S(2)}) async-start(bf16[8,40,512]{2,1,0:T(8,128)(2,1)} %maximum_maximum_fusion), calls=%async_computation | async-start | bytes 655360 | tf_op jit(solution)/shard_map/all_to_all | solution.py:205
  17.8 18.6 %collective-permute-start = (bf16[4,128,256]{2,1,0:T(8,128)(2,1)S(1)}, bf16[4,128,256]{2,1,0:T(8,128)(2,1)S(1)}, u32[]{:S(2)}, u32[]{:S(2)}) collective-permute-start(bf16[4,128,256]{2,1,0:T(8,128)(2,1)S(1)} %bitcast.27), channel_id=1, source_target_pairs={{0,4},{4,8},{8,12},{12,14},{14,10},{10,6},{6,2},{2,0},{1,5},{5,9},... | collective-permute-start | bytes 786440 | tf_op jit(solution)/shard_map/ppermute | solution.py:230
  19.8 20.6 %collective-permute-start.1 = (bf16[4,128,256]{2,1,0:T(8,128)(2,1)S(1)}, bf16[4,128,256]{2,1,0:T(8,128)(2,1)S(1)}, u32[]{:S(2)}, u32[]{:S(2)}) collective-permute-start(bf16[4,128,256]{2,1,0:T(8,128)(2,1)S(1)} %bitcast.28), channel_id=1, source_target_pairs={{4,0},{8,4},{12,8},{14,12},{10,14},{6,10},{2,6},{0,2},{5,1},{9,5},... | collective-permute-start | bytes 786440 | tf_op jit(solution)/shard_map/ppermute | solution.py:234
  36.4 9.8 %collective-permute-start.2 = (bf16[4,128,256]{2,1,0:T(8,128)(2,1)S(1)}, bf16[4,128,256]{2,1,0:T(8,128)(2,1)S(1)}, u32[]{:S(2)}, u32[]{:S(2)}) collective-permute-start(bf16[4,128,256]{2,1,0:T(8,128)(2,1)S(1)} %collective-permute-done.refs_1_), channel_id=1, source_target_pairs={{0,4},{4,8},{8,12},{12,14},{14,10},{10,6},{6,2},{2,0},{1,5},{5,9},... | collective-permute-start | bytes 786440 | tf_op jit(solution)/shard_map/ppermute | solution.py:230
  40.4 14.4 %collective-permute-start.3 = (bf16[4,128,256]{2,1,0:T(8,128)(2,1)S(1)}, bf16[4,128,256]{2,1,0:T(8,128)(2,1)S(1)}, u32[]{:S(2)}, u32[]{:S(2)}) collective-permute-start(bf16[4,128,256]{2,1,0:T(8,128)(2,1)S(1)} %collective-permute-done.1.refs_2_), channel_id=1, source_target_pairs={{4,0},{8,4},{12,8},{14,12},{10,14},{6,10},{2,6},{0,2},{5,1},{9,5},... | collective-permute-start | bytes 786440 | tf_op jit(solution)/shard_map/ppermute | solution.py:234
  46.2 16.9 %collective-permute-start.4 = (bf16[4,128,256]{2,1,0:T(8,128)(2,1)S(1)}, bf16[4,128,256]{2,1,0:T(8,128)(2,1)S(1)}, u32[]{:S(2)}, u32[]{:S(2)}) collective-permute-start(bf16[4,128,256]{2,1,0:T(8,128)(2,1)S(1)} %collective-permute-done.2.refs_3_), channel_id=1, source_target_pairs={{0,4},{4,8},{8,12},{12,14},{14,10},{10,6},{6,2},{2,0},{1,5},{5,9},... | collective-permute-start | bytes 786440 | tf_op jit(solution)/shard_map/ppermute | solution.py:230
  53.6 16.2 %collective-permute-start.8 = (bf16[256,512]{1,0:T(8,128)(2,1)S(1)}, bf16[256,512]{1,0:T(8,128)(2,1)S(1)}, u32[]{:S(2)}, u32[]{:S(2)}) collective-permute-start(bf16[256,512]{1,0:T(8,128)(2,1)S(1)} %fusion.3.refs_8_.refs_1_), channel_id=1, source_target_pairs={{0,16},{16,0},{1,17},{17,1},{2,18},{18,2},{3,19},{19,3},{4,20},{20... | collective-permute-start | bytes 786440 | tf_op jit(solution)/shard_map/ppermute | solution.py:169
  54.8 16.4 %collective-permute-start.5 = (bf16[4,128,256]{2,1,0:T(8,128)(2,1)S(1)}, bf16[4,128,256]{2,1,0:T(8,128)(2,1)S(1)}, u32[]{:S(2)}, u32[]{:S(2)}) collective-permute-start(bf16[4,128,256]{2,1,0:T(8,128)(2,1)S(1)} %collective-permute-done.3.refs_4_), channel_id=1, source_target_pairs={{4,0},{8,4},{12,8},{14,12},{10,14},{6,10},{2,6},{0,2},{5,1},{9,5},... | collective-permute-start | bytes 786440 | tf_op jit(solution)/shard_map/ppermute | solution.py:234
  54.8 16.4 %collective-permute-start.7 = (bf16[256,512]{1,0:T(8,128)(2,1)S(1)}, bf16[256,512]{1,0:T(8,128)(2,1)S(1)}, u32[]{:S(2)}, u32[]{:S(2)}) collective-permute-start(bf16[256,512]{1,0:T(8,128)(2,1)S(1)} %fusion.3.refs_8_.refs_1_), channel_id=1, source_target_pairs={{0,1},{1,0},{2,3},{3,2},{4,5},{5,4},{6,7},{7,6},{8,9},{9,8},{10,11... | collective-permute-start | bytes 786440 | tf_op jit(solution)/shard_map/ppermute | solution.py:169
  63.1 14.0 %collective-permute-start.6 = (bf16[4,128,256]{2,1,0:T(8,128)(2,1)S(1)}, bf16[4,128,256]{2,1,0:T(8,128)(2,1)S(1)}, u32[]{:S(2)}, u32[]{:S(2)}) collective-permute-start(bf16[4,128,256]{2,1,0:T(8,128)(2,1)S(1)} %collective-permute-done.4.refs_5_), channel_id=1, source_target_pairs={{0,4},{4,8},{8,12},{12,14},{14,10},{10,6},{6,2},{2,0},{1,5},{5,9},... | collective-permute-start | bytes 786440 | tf_op jit(solution)/shard_map/ppermute | solution.py:230
  69.8 9.4 %copy-start.2 = (bf16[256,512]{1,0:T(8,128)(2,1)}, bf16[256,512]{1,0:T(8,128)(2,1)S(1)}, u32[]{:S(2)}) copy-start(bf16[256,512]{1,0:T(8,128)(2,1)S(1)} %collective-permute-done.8.refs_10_.refs_3_) | copy-start | bytes 786436
  69.8 7.3 %collective-permute-start.9 = (bf16[256,512]{1,0:T(8,128)(2,1)S(1)}, bf16[256,512]{1,0:T(8,128)(2,1)S(1)}, u32[]{:S(2)}, u32[]{:S(2)}) collective-permute-start(bf16[256,512]{1,0:T(8,128)(2,1)S(1)} %collective-permute-done.8.refs_10_.refs_3_), channel_id=1, source_target_pairs={{0,1},{1,0},{2,3},{3,2},{4,5},{5,4},{6,7},{7,6},{8,9},{9,8},{10,11... | collective-permute-start | bytes 786440 | tf_op jit(solution)/shard_map/ppermute | solution.py:169
  71.2 8.0 %copy-start.4 = (bf16[256,512]{1,0:T(8,128)(2,1)}, bf16[256,512]{1,0:T(8,128)(2,1)S(1)}, u32[]{:S(2)}) copy-start(bf16[256,512]{1,0:T(8,128)(2,1)S(1)} %collective-permute-done.7.refs_9_.refs_2_) | copy-start | bytes 786436
  77.1 2.1 %copy-start.6 = (bf16[256,512]{1,0:T(8,128)(2,1)}, bf16[256,512]{1,0:T(8,128)(2,1)S(1)}, u32[]{:S(2)}) copy-start(bf16[256,512]{1,0:T(8,128)(2,1)S(1)} %collective-permute-done.9.refs_11_.refs_4_) | copy-start | bytes 786436
  79.2 9.3 %copy-start = (f32[256]{0:T(256)S(1)}, f32[256]{0:T(256)}, u32[]{:S(2)}) copy-start(f32[256]{0:T(256)} %param.12) | copy-start | bytes 3076
  79.2 9.2 %collective-permute-start.10 = (bf16[4,256,256]{2,1,0:T(8,128)(2,1)S(1)}, bf16[4,256,256]{2,1,0:T(8,128)(2,1)S(1)}, u32[]{:S(2)}, u32[]{:S(2)}) collective-permute-start(bf16[4,256,256]{2,1,0:T(8,128)(2,1)S(1)} %get-tuple-element.11), channel_id=1, source_target_pairs={{0,16},{16,0},{1,17},{17,1},{2,18},{18,2},{3,19},{19,3},{4,20},{20... | collective-permute-start | bytes 1572872 | tf_op jit(solution)/shard_map/ppermute | solution.py:169
  90.2 9.4 %collective-permute-start.11 = (bf16[10,256,256]{2,1,0:T(8,128)(2,1)S(1)}, bf16[10,256,256]{2,1,0:T(8,128)(2,1)S(1)}, u32[]{:S(2)}, u32[]{:S(2)}) collective-permute-start(bf16[10,256,256]{2,1,0:T(8,128)(2,1)S(1)} %get-tuple-element.13.mine_ref), channel_id=1, source_target_pairs={{0,1},{1,0},{2,3},{3,2},{4,5},{5,4},{6,7},{7,6},{8,9},{9,8},{10,11... | collective-permute-start | bytes 3932168 | tf_op jit(solution)/shard_map/ppermute | solution.py:169
  90.3 9.4 %collective-permute-start.12 = (bf16[3,256,256]{2,1,0:T(8,128)(2,1)}, bf16[3,256,256]{2,1,0:T(8,128)(2,1)}, u32[]{:S(2)}, u32[]{:S(2)}) collective-permute-start(bf16[3,256,256]{2,1,0:T(8,128)(2,1)} %res_mine_ref.1), channel_id=1, source_target_pairs={{0,1},{1,0},{2,3},{3,2},{4,5},{5,4},{6,7},{7,6},{8,9},{9,8},{10,11... | collective-permute-start | bytes 1179656 | tf_op jit(solution)/shard_map/ppermute | solution.py:169
  90.8 1.6 %copy-start.1 = (bf16[32,128,256]{2,1,0:T(8,128)(2,1)S(1)}, bf16[32,128,256]{2,1,0:T(8,128)(2,1)}, u32[]{:S(2)}) copy-start(bf16[32,128,256]{2,1,0:T(8,128)(2,1)} %all-gather.3.cloned.1.call-done) | copy-start | bytes 6291460
  92.4 0.9 copy-start.3
  93.3 0.9 copy-start.5
  94.3 0.9 copy-start.7
  95.2 4.5 %copy-start.8 = (bf16[256,256]{1,0:T(8,128)(2,1)S(1)}, bf16[256,256]{1,0:T(8,128)(2,1)}, u32[]{:S(2)}) copy-start(bf16[256,256]{1,0:T(8,128)(2,1)} %skip_ref.1) | copy-start | bytes 393220
  95.2 4.5 %copy-start.9 = (f32[256]{0:T(256)S(1)}, f32[256]{0:T(256)}, u32[]{:S(2)}) copy-start(f32[256]{0:T(256)} %param.17) | copy-start | bytes 3076
  95.2 4.5 %copy-start.10 = (f32[256]{0:T(256)S(1)}, f32[256]{0:T(256)}, u32[]{:S(2)}) copy-start(f32[256]{0:T(256)} %param.19) | copy-start | bytes 3076
  98.1 14.2 %collective-permute-start.13 = (bf16[4,256,256]{2,1,0:T(8,128)(2,1)}, bf16[4,256,256]{2,1,0:T(8,128)(2,1)}, u32[]{:S(2)}, u32[]{:S(2)}) collective-permute-start(bf16[4,256,256]{2,1,0:T(8,128)(2,1)} %get-tuple-element.14), channel_id=1, source_target_pairs={{0,16},{16,0},{1,17},{17,1},{2,18},{18,2},{3,19},{19,3},{4,20},{20... | collective-permute-start | bytes 1572872 | tf_op jit(solution)/shard_map/ppermute | solution.py:169
Sparse Core Ops, SparseCore 0:
  10.7 61.5 all-gather.2
where the time goes:
time: 124 us; the launch traced here: 123 us
  waiting for transfers between devices  51.2 us (41%)
  starting transfers between devices  32.3 us (26%)
  between operations  14.3 us (12%)
  Pallas kernels  12.9 us (10%)
  local copies, waits for them, and re-layouts  10 us (8%)
  other arithmetic  2.28 us (2%)
    ppermute x4, waiting for transfers between devices, gather_ring(): item = lax.ppermute(item, 'streams', onward)  36.5 us
    ppermute x4, starting transfers between devices, gather_ring(): item = lax.ppermute(item, 'streams', onward)  20 us
    ppermute x7, waiting for transfers between devices, swap(): return lax.ppermute(value, axis, [(0, 1), (1, 0)])  13.3 us
    unnamed x37, local copies, waits for them, and re-layouts  8.38 us
    all_to_all x1, starting transfers between devices, local(): lax.all_to_all(parcel, 'streams', split_axis=0, concat_axis=0, tiled=True)  7.25 us
    pallas_call x1, Pallas kernels, residual(): pl.pallas_call(residual_kernel, out_shape=jax.ShapeDtypeStruct(up.shape,...  6.13 us
    pallas_call x2, Pallas kernels, spread_taps(): pl.pallas_call(functools.partial(spread_kernel, count, steps), out_shape=...  4.97 us
    ppermute x7, starting transfers between devices, swap(): return lax.ppermute(value, axis, [(0, 1), (1, 0)])  4.85 us
  transfers between devices with their start and end apart: 16, of which 7 were waited for; matrix products, arithmetic and copies ran while one was open for 2% of the time, Pallas kernels for 10%

commit v1 on v0

v1 whole, which is shorter than its diff:
```python
import functools

import jax
import jax.numpy as jnp
from jax import lax
from jax.experimental import pallas as pl
from jax.experimental.pallas import tpu as pltpu
from jax.sharding import PartitionSpec as P

VMEM_LIMIT = 48 * 1024 * 1024
F32 = jnp.float32
BF16 = jnp.bfloat16
VMEM = pl.BlockSpec(memory_space=pltpu.VMEM)


def apply_elu(values):
    return jnp.where(values > 0, values, jnp.exp(jnp.minimum(values, 0.0)) - 1.0)


def ring_order(count):
    return [2 * p if p < count // 2 else 2 * (count - 1 - p) + 1 for p in range(count)]


def ring_place(stream, count):
    return jnp.where(stream % 2 == 0, stream // 2, count - 1 - stream // 2)


def ring_stream(place, count):
    return jnp.where(place < count // 2, 2 * place, 2 * (count - 1 - place) + 1)


def spread_kernel(count, steps, *refs):
    blocks = refs[: len(steps)]
    sides, (home_ref, away_ref) = refs[len(steps) : len(steps) + 4], refs[len(steps) + 4 : -3]
    kernel_rows, inputs, sems = refs[-3:]
    taps = kernel_rows.shape[0]
    rows = blocks[0].shape[-2]
    core = lax.axis_index("segment")
    place = ring_place(lax.axis_index("streams"), count)
    copies = []
    for slot, (step, block) in enumerate(zip(steps, blocks)):
        if step is None:
            source, target = block, kernel_rows
        else:
            distance, passed = step
            taker = 1 - core if passed else core
            stream = ring_stream(
                lax.rem(place + (2 * taker - 1) * distance + count, count), count
            )
            source = block if len(block.shape) == 3 else block.at[0]
            part = source.shape[0]
            first = 0 if part == taps else taker * part
            target = kernel_rows.at[
                pl.ds(first, part), pl.ds(pl.multiple_of(stream * rows, rows), rows), :
            ]
        copy = pltpu.make_async_copy(source, target, sems.at[slot])
        copy.start()
        copies.append(copy)
    half = sides[0].shape[1]
    for index, side in enumerate(sides):
        column = core if index % 2 == 0 else 1 - core
        inputs[index // 2, :, pl.ds(pl.multiple_of(column * half, half), half)] = side[...]
    for copy in copies:
        copy.wait()

    @pl.loop(0, taps)
    def _(tap):
        weights = kernel_rows[tap]
        home_ref[tap] = jnp.dot(inputs[0], weights, preferred_element_type=F32).astype(
            home_ref.dtype
        )
        away_ref[tap] = jnp.dot(inputs[1], weights, preferred_element_type=F32).astype(
            away_ref.dtype
        )


def spread_taps(sides, blocks, steps, count, home_type):
    taps, _, width = blocks[0].shape
    sessions, depth = sides[0].shape[0], 2 * sides[0].shape[1]
    return pl.pallas_call(
        functools.partial(spread_kernel, count, steps),
        out_shape=(
            jax.ShapeDtypeStruct((taps, sessions, width), home_type),
            jax.ShapeDtypeStruct((taps, sessions, width), BF16),
        ),
        in_specs=[pl.BlockSpec(memory_space=pl.ANY)] * len(blocks) + [VMEM] * 4,
        out_specs=(VMEM, VMEM),
        scratch_shapes=[
            pltpu.VMEM((taps, depth, width), BF16),
            pltpu.VMEM((2, sessions, depth), BF16),
            pltpu.SemaphoreType.DMA((len(blocks),)),
        ],
        compiler_params=pltpu.CompilerParams(vmem_limit_bytes=VMEM_LIMIT),
        cost_estimate=pl.CostEstimate(
            flops=4 * taps * sessions * depth * width,
            bytes_accessed=2 * taps * depth * width + 4 * sessions * depth + 6 * taps * sessions * width,
            transcendentals=0,
        ),
    )(*blocks, *sides)


def excite_kernel(group_ref, own_ref, other_ref, prev_ref, bias_ref, up_ref, window_ref):
    taps = own_ref.shape[0]
    bias = bias_ref[...]
    group = group_ref[0]
    history = prev_ref.shape[0] - 2 * taps
    for step in range(history):
        window_ref[step] = prev_ref[2 * taps + step]
    for half in range(2):
        for tap in range(taps):
            value = jnp.where(group == half, own_ref[tap], other_ref[tap].astype(F32))
            step = half * taps + tap
            up = value + prev_ref[step].astype(F32) + bias
            up_ref[step] = up
            window_ref[history + step] = apply_elu(up).astype(BF16)


def excite(group, own, other, prev, bias):
    taps, sessions, width = own.shape
    return pl.pallas_call(
        excite_kernel,
        out_shape=(
            jax.ShapeDtypeStruct((2 * taps, sessions, width), F32),
            jax.ShapeDtypeStruct((prev.shape[0], sessions, width), BF16),
        ),
        in_specs=[pl.BlockSpec(memory_space=pltpu.SMEM), VMEM, VMEM, VMEM, VMEM],
        out_specs=(VMEM, VMEM),
        compiler_params=pltpu.CompilerParams(vmem_limit_bytes=VMEM_LIMIT),
        cost_estimate=pl.CostEstimate(
            flops=20 * taps * sessions * width,
            bytes_accessed=40 * taps * sessions * width,
            transcendentals=2 * taps * sessions * width,
        ),
    )(group, own, other, prev, bias)


def residual_kernel(
    up_ref, mine_ref, theirs_ref, res_mine_ref, res_theirs_ref, res_bias_ref, skip_ref, skip_bias_ref, out_ref, frames
):
    steps, block, width = up_ref.shape
    branch = None
    for source, weights in ((mine_ref, res_mine_ref), (theirs_ref, res_theirs_ref)):
        for offset in range(weights.shape[0]):
            term = jnp.dot(
                source[offset : offset + steps].reshape(steps * block, width),
                weights[offset],
                preferred_element_type=F32,
            )
            branch = term if branch is None else branch + term
    hidden = apply_elu(branch + res_bias_ref[...]).astype(BF16)
    projected = jnp.dot(hidden, skip_ref[...], preferred_element_type=F32)
    mixed = up_ref[...] + projected.reshape(steps, block, width) + skip_bias_ref[...]
    for step in range(steps):
        for part in range(width // 128):
            frames.at[part][pl.ds(step, block, stride=steps), :] = mixed[
                step, :, part * 128 : (part + 1) * 128
            ]
    for part in range(width // 128):
        out_ref[:, part * 128 : (part + 1) * 128] = frames[part].astype(BF16)


def residual(up, mine, theirs, res_mine, res_theirs, res_bias, skip_weight, skip_bias):
    steps, sessions, width = up.shape
    window, block = mine.shape[0], sessions // 4
    frames = pl.BlockSpec((window, block, width), lambda i: (0, i, 0))
    return pl.pallas_call(
        residual_kernel,
        out_shape=jax.ShapeDtypeStruct((sessions * steps, width), BF16),
        grid=(4,),
        in_specs=[pl.BlockSpec((steps, block, width), lambda i: (0, i, 0)), frames, frames]
        + [VMEM] * 5,
        out_specs=pl.BlockSpec((block * steps, width), lambda i: (i, 0)),
        scratch_shapes=[pltpu.VMEM((width // 128, block * steps, 128), F32)],
        compiler_params=pltpu.CompilerParams(vmem_limit_bytes=VMEM_LIMIT),
        cost_estimate=pl.CostEstimate(
            flops=2 * up.size * (2 * res_mine.shape[0] + 1) * res_mine.shape[2],
            bytes_accessed=12 * up.size,
            transcendentals=up.size,
        ),
    )(up, mine, theirs, res_mine, res_theirs, res_bias, skip_weight, skip_bias)


def weave_kernel(group_ref, *refs):
    owns, others, (out_ref, frames) = refs[: len(refs) // 2 - 1], refs[len(refs) // 2 - 1 : -2], refs[-2:]
    group = group_ref[0]
    block, width = owns[0].shape[1:]
    steps = frames.shape[1] // block
    for half in range(2):
        step = half * steps // 2
        for own, other in zip(owns, others):
            for tap in range(own.shape[0]):
                value = jnp.where(group == half, own[tap].astype(F32), other[tap].astype(F32))
                for part in range(width // 128):
                    frames.at[part][pl.ds(step, block, stride=steps), :] = value[
                        :, part * 128 : (part + 1) * 128
                    ]
                step += 1
    for part in range(width // 128):
        out_ref[:, part * 128 : (part + 1) * 128] = frames[part].astype(BF16)


def weave(group, owns, others):
    sessions, width = owns[0].shape[1:]
    steps, block = 2 * sum(own.shape[0] for own in owns), sessions // 4
    taps = [
        pl.BlockSpec((own.shape[0], block, width), lambda i: (0, i, 0)) for own in owns + others
    ]
    return pl.pallas_call(
        weave_kernel,
        out_shape=jax.ShapeDtypeStruct((sessions * steps, width), BF16),
        grid=(4,),
        in_specs=[pl.BlockSpec(memory_space=pltpu.SMEM)] + taps,
        out_specs=pl.BlockSpec((block * steps, width), lambda i: (i, 0)),
        scratch_shapes=[pltpu.VMEM((width // 128, block * steps, 128), F32)],
        compiler_params=pltpu.CompilerParams(vmem_limit_bytes=VMEM_LIMIT),
        cost_estimate=pl.CostEstimate(
            flops=0, bytes_accessed=4 * sessions * steps * width, transcendentals=0
        ),
    )(group, *owns, *others)


def swap(value, axis):
    return lax.ppermute(value, axis, [(0, 1), (1, 0)])


def after(value, earlier):
    return lax.optimization_barrier((value, earlier))[0]


class Ring:
    def __init__(self, count, own, other):
        order = ring_order(count)
        self.count = count
        self.pairs = []
        for p in range(count):
            here, there = order[p], order[(p + 1) % count]
            self.pairs += [(2 * here, 2 * there), (2 * there + 1, 2 * here + 1)]
        self.item = jnp.stack([own, other])
        self.blocks, self.steps, self.rounds = [own], [(0, 0)], 0

    def round(self, earlier=None):
        self.rounds += 1
        item = self.item
        if 2 * self.rounds == self.count:
            part = item.shape[1] // 2
            item = lax.dynamic_slice_in_dim(item, lax.axis_index("segment") * part, part, axis=1)
        if earlier is not None:
            item = after(item, earlier)
        item = lax.ppermute(item, ("streams", "segment"), self.pairs)
        self.item = item
        self.blocks += [item, swap(item[1], "segment")]
        self.steps += [(self.rounds, 0), (self.rounds, 1)]
        return item


def local(
    count,
    latent,
    conv_weight,
    conv_bias,
    tail_cache,
    input_cache,
    resume_slot,
    res_weight,
    res_bias,
    skip_weight,
    skip_bias,
):
    group = lax.axis_index("groups")
    group_word = group[None].astype(jnp.int32)
    rows, tap_count, width = conv_weight.shape
    sessions = latent.shape[0]
    taps = tap_count // 4

    halves = []
    for first in (0, tap_count // 2):
        part = lax.dynamic_slice_in_dim(conv_weight, first + group * taps, taps, axis=1)
        halves.append(part.transpose(1, 0, 2))
    own = jnp.concatenate(halves, axis=0)
    cuts = ((0, taps), (taps, taps + taps // 2), (taps + taps // 2, 2 * taps))

    if rows % 128 == 0 and count % 2 == 0:
        other = swap(own, "segment")
        rings = [Ring(count, own[a:b], other[a:b]) for a, b in cuts]
        up_ring, first_ring, second_ring = rings
        first_done = up_ring.round()
        first_ring.round()
        last = first_done
        for r in range(2, count // 2 + 1):
            behind = last
            last = up_ring.round()
            first_ring.round()
            if r >= 3:
                second_ring.round(behind)
        while second_ring.rounds < count // 2:
            second_ring.round()
        gathered = [(ring.blocks, ring.steps) for ring in rings]
    else:
        gathered = [
            ([lax.all_gather(own[a:b], "streams", axis=1, tiled=True)], [None]) for a, b in cuts
        ]
        first_done = own

    portion = sessions // count
    cap = tail_cache.shape[0] // count
    half_taps, history = tail_cache.shape[1], input_cache.shape[1]
    slot_step = jnp.broadcast_to(
        resume_slot.astype(BF16)[:, None, None], (count * cap, 1, width)
    )
    filler = jnp.zeros((count * cap, half_taps - history - 1, width), BF16)
    beside = jnp.concatenate([input_cache, slot_step, filler], axis=1)
    stored = jnp.concatenate([tail_cache, beside], axis=2).reshape(count, cap * half_taps, 2 * width)
    parcel = jnp.concatenate([latent.reshape(count, portion, 2 * width), stored], axis=1)
    parcel = after(parcel, first_done)
    parcel = lax.all_to_all(parcel, "streams", split_axis=0, concat_axis=0, tiled=True)
    handed = parcel[:, :portion].reshape(sessions, 2 * width)
    stored = parcel[:, portion:].reshape(count * cap, half_taps, 2 * width)

    near_half = apply_elu(handed.astype(F32)).astype(BF16)
    far_half = swap(near_half, "groups")
    sides = (near_half, swap(near_half, "segment"), far_half, swap(far_half, "segment"))

    slots = stored[:, history, width:].astype(jnp.int32)[:, :1]
    one_hot = (slots == jnp.arange(sessions, dtype=jnp.int32)[None, :]).astype(BF16)
    packed = jnp.concatenate([stored[:, :, :width], stored[:, :history, width:]], axis=1)
    prev = jnp.einsum("js,jkc->ksc", one_hot, packed, preferred_element_type=F32).astype(BF16)

    res_theirs = swap(res_weight, "segment")

    own_up, away_up = spread_taps(sides, *gathered[0], count, F32)
    other_up = swap(away_up, "groups")
    owns, others = [], []
    for blocks, steps in gathered[1:]:
        own_tail, away_tail = spread_taps(sides, blocks, steps, count, BF16)
        owns.append(own_tail)
        others.append(swap(away_tail, "groups"))

    up, mine = excite(group_word, own_up, other_up, prev, conv_bias[None])
    theirs = swap(mine, "segment")
    decoded = residual(
        up, mine, theirs, res_weight, res_theirs, res_bias[None], skip_weight, skip_bias[None]
    )
    decoded, others[-1] = lax.optimization_barrier((decoded, others[-1]))
    new_tail = weave(group_word, owns, others)
    shape = (sessions, half_taps, width)
    return decoded.reshape(shape), new_tail.reshape(shape)


def solution(mesh):
    placed = (
        P(("groups", "streams"), "segment"),
        P("streams", None, "segment"),
        P("segment"),
        P(("groups", "streams"), None, "segment"),
        P(("groups", "streams"), None, "segment"),
        P(("groups", "streams")),
        P(None, "segment", None),
        P(),
        P(None, "segment"),
        P("segment"),
    )
    return jax.shard_map(
        functools.partial(local, mesh.shape["streams"]),
        mesh=mesh,
        in_specs=placed,
        out_specs=(
            P(("groups", "streams"), None, "segment"),
            P(("groups", "streams"), None, "segment"),
        ),
        check_vma=False,
    )
```

time: 124 us -> 98.1 us (0.79)
  waiting for transfers between devices: 51.2 us -> 32.8 us
  between operations: 14.3 us -> 1.07 us
  starting transfers between devices: 32.3 us -> 43.9 us
  local copies, waits for them, and re-layouts: 10 us -> 3.35 us
  Pallas kernels: 12.9 us -> 14.3 us
    ppermute x7 -> x12, waiting for transfers between devices: 37.8 us -> 22.3 us  [round(): item = lax.ppermute(item, ('streams', 'segment'), self.pairs)]
    ppermute x7 -> x12, starting transfers between devices: 20.1 us -> 30.9 us  [round(): item = lax.ppermute(item, ('streams', 'segment'), self.pairs)]
    unnamed x37 -> x29, local copies, waits for them, and re-layouts: 8.38 us -> 0.15 us
    ppermute x7 -> x21, starting transfers between devices: 4.85 us -> 9.13 us  [swap(): return lax.ppermute(value, axis, [(0, 1), (1, 0)])]
    all_to_all x1, starting transfers between devices: 7.25 us -> 3.78 us  [local(): lax.all_to_all(parcel, 'streams', split_axis=0, concat_axis=0, tiled=True)]
    ppermute x7 -> x21, waiting for transfers between devices: 13.3 us -> 10.5 us  [swap(): return lax.ppermute(value, axis, [(0, 1), (1, 0)])]
    squeeze x0 -> x12, local copies, waits for them, and re-layouts: none -> 1.48 us  [round(): self.blocks += [item, swap(item[1], 'segment')]]
    pallas_call x2 -> x3, Pallas kernels: 4.97 us -> 5.99 us  [spread_taps(): pl.pallas_call(functools.partial(spread_kernel, count, steps), out_shape=...]
  transfers between devices with their start and end apart: 16 -> 34, of which waited for: 7 -> 14; matrix products, arithmetic and copies ran while one was open for 2% -> 4% of each run, Pallas kernels for 10% -> 12%
where the time goes in v1:
time: 98.1 us; the launch traced here: 97.9 us
  starting transfers between devices  43.9 us (45%)
  waiting for transfers between devices  32.8 us (33%)
  Pallas kernels  14.3 us (15%)
  local copies, waits for them, and re-layouts  3.35 us (3%)
  other arithmetic  1.92 us (2%)
  between operations  1.07 us (1%)
    ppermute x12, starting transfers between devices, round(): item = lax.ppermute(item, ('streams', 'segment'), self.pairs)  30.9 us
    ppermute x12, waiting for transfers between devices, round(): item = lax.ppermute(item, ('streams', 'segment'), self.pairs)  22.3 us
    ppermute x21, waiting for transfers between devices, swap(): return lax.ppermute(value, axis, [(0, 1), (1, 0)])  10.5 us
    ppermute x21, starting transfers between devices, swap(): return lax.ppermute(value, axis, [(0, 1), (1, 0)])  9.13 us
    pallas_call x3, Pallas kernels, spread_taps(): pl.pallas_call(functools.partial(spread_kernel, count, steps), out_shape=...  5.99 us
    pallas_call x1, Pallas kernels, residual(): pl.pallas_call(residual_kernel, out_shape=jax.ShapeDtypeStruct((sessions...  4.48 us
    all_to_all x1, starting transfers between devices, local(): lax.all_to_all(parcel, 'streams', split_axis=0, concat_axis=0, tiled=True)  3.78 us
    pallas_call x1, Pallas kernels, weave(): pl.pallas_call(weave_kernel, out_shape=jax.ShapeDtypeStruct((sessions * s...  2.04 us
  transfers between devices with their start and end apart: 34, of which 14 were waited for; matrix products, arithmetic and copies ran while one was open for 4% of the time, Pallas kernels for 12%

profile of v1, /device:TPU:0, one launch (start us, length us, event | category | flops | bytes accessed | tf_op | source)
XLA Modules:
  0.0 97.9 jit_solution(5672445670350542668)
XLA Ops:
  0.6 1.5 %constant_dynamic-slice_fusion.3 = (bf16[128,4,256]{2,1,0:T(4,128)(2,1)S(1)}, bf16[128,4,256]{2,1,0:T(4,128)(2,1)S(1)}) fusion(bf16[128,16,256]{2,1,0:T(8,128)(2,1)} %param.11, s32[]{:T(128)S(6)} %select_n.18, s32[]{:T(128)S(6)} %select_n.17), kind=kLoop, calls=%fused_computation.41 | loop fusion | bytes 1048584 | tf_op jit(solution)/shard_map/dynamic_slice | solution.py:277
  2.3 0.5 collective-permute-start
  2.8 1.5 %collective-permute-done = bf16[8,128,256]{2,1,0:T(8,128)(2,1)S(1)} collective-permute-done((bf16[8,128,256]{2,1,0:T(8,128)(2,1)S(1)}, bf16[8,128,256]{2,1,0:T(8,128)(2,1)S(1)}, u32[]{:S(2)}, u32[]{:S(2)}) %collective-permute-start) | collective-permute-done | bytes 524320 | tf_op jit(solution)/shard_map/ppermute | solution.py:223
  4.4 3.0 %collective-permute-start.1 = (bf16[2,4,128,256]{3,2,1,0:T(8,128)(2,1)S(1)}, bf16[2,4,128,256]{3,2,1,0:T(8,128)(2,1)S(1)}, u32[]{:S(2)}, u32[]{:S(2)}) collective-permute-start(bf16[2,4,128,256]{3,2,1,0:T(8,128)(2,1)S(1)} %pad_maximum_fusion.1), channel_id=1, source_target_pairs={{0,4},{5,1},{4,8},{9,5},{8,12},{13,9},{12,14},{15,13},{14,10},{11,... | collective-permute-start | bytes 1572872 | tf_op jit(solution)/shard_map/ppermute | solution.py:249
  7.5 7.0 %collective-permute-done.1.refs_1_ = bf16[2,4,128,256]{3,2,1,0:T(8,128)(2,1)S(1)} collective-permute-done((bf16[2,4,128,256]{3,2,1,0:T(8,128)(2,1)S(1)}, bf16[2,4,128,256]{3,2,1,0:T(8,128)(2,1)S(1)}, u32[]{:S(2)}, u32[]{:S(2)}) %collective-permute-start.1) | collective-permute-done | bytes 524320 | tf_op jit(solution)/shard_map/ppermute | solution.py:249
  14.5 2.1 %collective-permute-start.3 = (bf16[2,4,128,256]{3,2,1,0:T(8,128)(2,1)S(1)}, bf16[2,4,128,256]{3,2,1,0:T(8,128)(2,1)S(1)}, u32[]{:S(2)}, u32[]{:S(2)}) collective-permute-start(bf16[2,4,128,256]{3,2,1,0:T(8,128)(2,1)S(1)} %collective-permute-done.1.refs_1_), channel_id=1, source_target_pairs={{0,4},{5,1},{4,8},{9,5},{8,12},{13,9},{12,14},{15,13},{14,10},{11,... | collective-permute-start | bytes 1572872 | tf_op jit(solution)/shard_map/ppermute | solution.py:249
  16.7 1.6 %collective-permute-start.24 = (bf16[2,2,128,256]{3,2,1,0:T(8,128)(2,1)S(1)}, bf16[2,2,128,256]{3,2,1,0:T(8,128)(2,1)S(1)}, u32[]{:S(2)}, u32[]{:S(2)}) collective-permute-start(bf16[2,2,128,256]{3,2,1,0:T(8,128)(2,1)S(1)} %pad_maximum_fusion.3), channel_id=1, source_target_pairs={{0,4},{5,1},{4,8},{9,5},{8,12},{13,9},{12,14},{15,13},{14,10},{11,... | collective-permute-start | bytes 786440 | tf_op jit(solution)/shard_map/ppermute | solution.py:249
  18.4 0.8 maximum_maximum_fusion
  19.2 3.8 %all-to-all-start = ((bf16[8,40,512]{2,1,0:T(8,128)(2,1)}), bf16[8,40,512]{2,1,0:T(8,128)(2,1)S(1)}, u32[]{:S(2)}, u32[]{:S(2)}) async-start(bf16[8,40,512]{2,1,0:T(8,128)(2,1)} %maximum_maximum_fusion), calls=%async_computation | async-start | bytes 655360 | tf_op jit(solution)/shard_map/all_to_all | solution.py:315
  23.0 0.7 pad_maximum_fusion.2
  23.7 5.1 %collective-permute-done.24.refs_1_ = bf16[2,2,128,256]{3,2,1,0:T(8,128)(2,1)S(1)} collective-permute-done((bf16[2,2,128,256]{3,2,1,0:T(8,128)(2,1)S(1)}, bf16[2,2,128,256]{3,2,1,0:T(8,128)(2,1)S(1)}, u32[]{:S(2)}, u32[]{:S(2)}) %collective-permute-start.24) | collective-permute-done | bytes 262176 | tf_op jit(solution)/shard_map/ppermute | solution.py:249
  28.8 3.4 %collective-permute-start.26 = (bf16[2,2,128,256]{3,2,1,0:T(8,128)(2,1)S(1)}, bf16[2,2,128,256]{3,2,1,0:T(8,128)(2,1)S(1)}, u32[]{:S(2)}, u32[]{:S(2)}) collective-permute-start(bf16[2,2,128,256]{3,2,1,0:T(8,128)(2,1)S(1)} %collective-permute-done.24.refs_1_), channel_id=1, source_target_pairs={{0,4},{5,1},{4,8},{9,5},{8,12},{13,9},{12,14},{15,13},{14,10},{11,... | collective-permute-start | bytes 786440 | tf_op jit(solution)/shard_map/ppermute | solution.py:249
  32.1 3.3 %collective-permute-start.5 = (bf16[2,4,128,256]{3,2,1,0:T(8,128)(2,1)S(1)}, bf16[2,4,128,256]{3,2,1,0:T(8,128)(2,1)S(1)}, u32[]{:S(2)}, u32[]{:S(2)}) collective-permute-start(bf16[2,4,128,256]{3,2,1,0:T(8,128)(2,1)S(1)} %collective-permute-done.3.refs_3_), channel_id=1, source_target_pairs={{0,4},{5,1},{4,8},{9,5},{8,12},{13,9},{12,14},{15,13},{14,10},{11,... | collective-permute-start | bytes 1572872 | tf_op jit(solution)/shard_map/ppermute | solution.py:249
  35.5 0.7 slice_bitcast_fusion.6
  36.1 0.7 slice_bitcast_fusion.2
  36.8 2.5 %collective-permute-start.28 = (bf16[2,2,128,256]{3,2,1,0:T(8,128)(2,1)S(1)}, bf16[2,2,128,256]{3,2,1,0:T(8,128)(2,1)S(1)}, u32[]{:S(2)}, u32[]{:S(2)}) collective-permute-start(bf16[2,2,128,256]{3,2,1,0:T(8,128)(2,1)S(1)} %collective-permute-done.26.refs_3_), channel_id=1, source_target_pairs={{0,4},{5,1},{4,8},{9,5},{8,12},{13,9},{12,14},{15,13},{14,10},{11,... | collective-permute-start | bytes 786440 | tf_op jit(solution)/shard_map/ppermute | solution.py:249
  39.5 1.6 %collective-permute-start.10 = (bf16[256,512]{1,0:T(8,128)(2,1)S(1)}, bf16[256,512]{1,0:T(8,128)(2,1)S(1)}, u32[]{:S(2)}, u32[]{:S(2)}) collective-permute-start(bf16[256,512]{1,0:T(8,128)(2,1)S(1)} %fusion.3.refs_9_), channel_id=1, source_target_pairs={{0,16},{16,0},{1,17},{17,1},{2,18},{18,2},{3,19},{19,3},{4,20},{20... | collective-permute-start | bytes 786440 | tf_op jit(solution)/shard_map/ppermute | solution.py:223
  41.1 1.0 %collective-permute-done.5.refs_5_ = bf16[2,4,128,256]{3,2,1,0:T(8,128)(2,1)S(1)} collective-permute-done((bf16[2,4,128,256]{3,2,1,0:T(8,128)(2,1)S(1)}, bf16[2,4,128,256]{3,2,1,0:T(8,128)(2,1)S(1)}, u32[]{:S(2)}, u32[]{:S(2)}) %collective-permute-start.5) | collective-permute-done | bytes 524320 | tf_op jit(solution)/shard_map/ppermute | solution.py:249
  42.2 2.9 %collective-permute-start.7 = (bf16[2,2,128,256]{3,2,1,0:T(8,128)(2,1)S(1)}, bf16[2,2,128,256]{3,2,1,0:T(8,128)(2,1)S(1)}, u32[]{:S(2)}, u32[]{:S(2)}) collective-permute-start(bf16[2,2,128,256]{3,2,1,0:T(8,128)(2,1)S(1)} %constant_dynamic-slice_fusion.2), channel_id=1, source_target_pairs={{0,4},{5,1},{4,8},{9,5},{8,12},{13,9},{12,14},{15,13},{14,10},{11,... | collective-permute-start | bytes 786440 | tf_op jit(solution)/shard_map/ppermute | solution.py:249
  45.2 0.8 collective-permute-done.10.refs_11_
  46.0 2.9 %collective-permute-done.7.refs_7_ = bf16[2,2,128,256]{3,2,1,0:T(8,128)(2,1)S(1)} collective-permute-done((bf16[2,2,128,256]{3,2,1,0:T(8,128)(2,1)S(1)}, bf16[2,2,128,256]{3,2,1,0:T(8,128)(2,1)S(1)}, u32[]{:S(2)}, u32[]{:S(2)}) %collective-permute-start.7) | collective-permute-done | bytes 262176 | tf_op jit(solution)/shard_map/ppermute | solution.py:249
  48.9 0.6 collective-permute-start.6
  49.7 0.5 collective-permute-start.25
  50.2 2.5 %collective-permute-start.30 = (bf16[2,1,128,256]{3,2,1,0:T(8,128)(2,1)S(1)}, bf16[2,1,128,256]{3,2,1,0:T(8,128)(2,1)S(1)}, u32[]{:S(2)}, u32[]{:S(2)}) collective-permute-start(bf16[2,1,128,256]{3,2,1,0:T(8,128)(2,1)S(1)} %constant_dynamic-slice_fusion), channel_id=1, source_target_pairs={{0,4},{5,1},{4,8},{9,5},{8,12},{13,9},{12,14},{15,13},{14,10},{11,... | collective-permute-start | bytes 393224 | tf_op jit(solution)/shard_map/ppermute | solution.py:249
  52.7 2.5 %collective-permute-start.15 = (bf16[2,2,128,256]{3,2,1,0:T(8,128)(2,1)S(1)}, bf16[2,2,128,256]{3,2,1,0:T(8,128)(2,1)S(1)}, u32[]{:S(2)}, u32[]{:S(2)}) collective-permute-start(bf16[2,2,128,256]{3,2,1,0:T(8,128)(2,1)S(1)} %copy-done.6), channel_id=1, source_target_pairs={{0,4},{5,1},{4,8},{9,5},{8,12},{13,9},{12,14},{15,13},{14,10},{11,... | collective-permute-start | bytes 786440 | tf_op jit(solution)/shard_map/ppermute | solution.py:249
  55.1 2.3 %shard_map.113 = (f32[4,256,256]{2,1,0:T(8,128)S(1)}, bf16[4,256,256]{2,1,0:T(8,128)(2,1)S(1)}) custom-call(bf16[4,128,256]{2,1,0:T(8,128)(2,1)S(1)} %bitcast.63, bf16[2,4,128,256]{3,2,1,0:T(8,128)(2,1)S(1)} %collective-permute-done.1.refs_1_, bf16[4,128,256]{2,1,0:T(8,128)(2,1)S(1)} %collective-permute-done.2.refs_2_, ...), custom_call_target="tpu_custom_call" | custom-call | flops 1073741824 | bytes 4718592 | tf_op jit(solution)/shard_map/pallas_call | solution.py:80
  57.4 1.6 %collective-permute-start.12 = (bf16[4,256,256]{2,1,0:T(8,128)(2,1)S(1)}, bf16[4,256,256]{2,1,0:T(8,128)(2,1)S(1)}, u32[]{:S(2)}, u32[]{:S(2)}) collective-permute-start(bf16[4,256,256]{2,1,0:T(8,128)(2,1)S(1)} %get-tuple-element.17), channel_id=1, source_target_pairs={{0,16},{16,0},{1,17},{17,1},{2,18},{18,2},{3,19},{19,3},{4,20},{20... | collective-permute-start | bytes 1572872 | tf_op jit(solution)/shard_map/ppermute | solution.py:223
  59.1 2.4 %collective-permute-start.17 = (bf16[2,2,128,256]{3,2,1,0:T(8,128)(2,1)S(1)}, bf16[2,2,128,256]{3,2,1,0:T(8,128)(2,1)S(1)}, u32[]{:S(2)}, u32[]{:S(2)}) collective-permute-start(bf16[2,2,128,256]{3,2,1,0:T(8,128)(2,1)S(1)} %collective-permute-done.15.refs_1_), channel_id=1, source_target_pairs={{0,4},{5,1},{4,8},{9,5},{8,12},{13,9},{12,14},{15,13},{14,10},{11,... | collective-permute-start | bytes 786440 | tf_op jit(solution)/shard_map/ppermute | solution.py:249
  61.7 0.6 fusion.prev_ref
  62.3 3.2 %collective-permute-done.17.refs_3_ = bf16[2,2,128,256]{3,2,1,0:T(8,128)(2,1)S(1)} collective-permute-done((bf16[2,2,128,256]{3,2,1,0:T(8,128)(2,1)S(1)}, bf16[2,2,128,256]{3,2,1,0:T(8,128)(2,1)S(1)}, u32[]{:S(2)}, u32[]{:S(2)}) %collective-permute-start.17) | collective-permute-done | bytes 262176 | tf_op jit(solution)/shard_map/ppermute | solution.py:249
  65.5 2.4 %collective-permute-start.19 = (bf16[2,2,128,256]{3,2,1,0:T(8,128)(2,1)S(1)}, bf16[2,2,128,256]{3,2,1,0:T(8,128)(2,1)S(1)}, u32[]{:S(2)}, u32[]{:S(2)}) collective-permute-start(bf16[2,2,128,256]{3,2,1,0:T(8,128)(2,1)S(1)} %collective-permute-done.17.refs_3_), channel_id=1, source_target_pairs={{0,4},{5,1},{4,8},{9,5},{8,12},{13,9},{12,14},{15,13},{14,10},{11,... | collective-permute-start | bytes 786440 | tf_op jit(solution)/shard_map/ppermute | solution.py:249
  67.9 1.1 %collective-permute-done.12.other_ref = bf16[4,256,256]{2,1,0:T(8,128)(2,1)S(1)} collective-permute-done((bf16[4,256,256]{2,1,0:T(8,128)(2,1)S(1)}, bf16[4,256,256]{2,1,0:T(8,128)(2,1)S(1)}, u32[]{:S(2)}, u32[]{:S(2)}) %collective-permute-start.12) | collective-permute-done | bytes 524320 | tf_op jit(solution)/shard_map/ppermute | solution.py:223
  69.0 1.8 %shard_map.114 = (f32[8,256,256]{2,1,0:T(8,128)}, bf16[10,256,256]{2,1,0:T(8,128)(2,1)S(1)}) custom-call(s32[1]{0:T(128)} %bitcast.group_ref, f32[4,256,256]{2,1,0:T(8,128)S(1)} %get-tuple-element.16.own_ref, bf16[4,256,256]{2,1,0:T(8,128)(2,1)S(1)} %collective-permute-done.12.other_ref, bf16[10,256,256]{2,1,0:T(8,128)(2,1)S(1)} %fusion.prev_ref, ...), custom_call_target="tpu_custom_call" | custom-call | flops 5242880 | bytes 10485760 | tf_op jit(solution)/shard_map/pallas_call | solution.py:120
  70.8 0.6 collective-permute-start.16
  71.4 0.5 collective-permute-done.19.refs_5_
  71.9 2.4 %collective-permute-start.21 = (bf16[2,1,128,256]{3,2,1,0:T(8,128)(2,1)S(1)}, bf16[2,1,128,256]{3,2,1,0:T(8,128)(2,1)S(1)}, u32[]{:S(2)}, u32[]{:S(2)}) collective-permute-start(bf16[2,1,128,256]{3,2,1,0:T(8,128)(2,1)S(1)} %constant_dynamic-slice_fusion.1), channel_id=1, source_target_pairs={{0,4},{5,1},{4,8},{9,5},{8,12},{13,9},{12,14},{15,13},{14,10},{11,... | collective-permute-start | bytes 393224 | tf_op jit(solution)/shard_map/ppermute | solution.py:249
  74.4 2.5 %collective-permute-done.21.refs_7_ = bf16[2,1,128,256]{3,2,1,0:T(8,128)(2,1)S(1)} collective-permute-done((bf16[2,1,128,256]{3,2,1,0:T(8,128)(2,1)S(1)}, bf16[2,1,128,256]{3,2,1,0:T(8,128)(2,1)S(1)}, u32[]{:S(2)}, u32[]{:S(2)}) %collective-permute-start.21) | collective-permute-done | bytes 131104 | tf_op jit(solution)/shard_map/ppermute | solution.py:249
  77.0 0.6 collective-permute-start.14
  77.6 0.4 collective-permute-start.29
  78.4 1.1 %collective-permute-done.22.refs_8_ = bf16[1,128,256]{2,1,0:T(8,128)(2,1)S(1)} collective-permute-done((bf16[1,128,256]{2,1,0:T(8,128)(2,1)S(1)}, bf16[1,128,256]{2,1,0:T(8,128)(2,1)S(1)}, u32[]{:S(2)}, u32[]{:S(2)}) %collective-permute-start.22) | collective-permute-done | bytes 65568 | tf_op jit(solution)/shard_map/ppermute | solution.py:223
  79.7 1.8 %shard_map.116 = (bf16[2,256,256]{2,1,0:T(8,128)(2,1)S(1)}, bf16[2,256,256]{2,1,0:T(8,128)(2,1)S(1)}) custom-call(bf16[2,128,256]{2,1,0:T(8,128)(2,1)S(1)} %get-tuple-element.35.refs_0_, bf16[2,2,128,256]{3,2,1,0:T(8,128)(2,1)S(1)} %collective-permute-done.15.refs_1_, bf16[2,128,256]{2,1,0:T(8,128)(2,1)S(1)} %collective-permute-done.16.refs_2_, ...), custom_call_target="tpu_custom_call" | custom-call | flops 536870912 | bytes 2883584 | tf_op jit(solution)/shard_map/pallas_call | solution.py:80
  81.6 1.5 %collective-permute-start.23 = (bf16[2,256,256]{2,1,0:T(8,128)(2,1)S(1)}, bf16[2,256,256]{2,1,0:T(8,128)(2,1)S(1)}, u32[]{:S(2)}, u32[]{:S(2)}) collective-permute-start(bf16[2,256,256]{2,1,0:T(8,128)(2,1)S(1)} %get-tuple-element.22), channel_id=1, source_target_pairs={{0,16},{16,0},{1,17},{17,1},{2,18},{18,2},{3,19},{19,3},{4,20},{20... | collective-permute-start | bytes 786440 | tf_op jit(solution)/shard_map/ppermute | solution.py:223
  83.1 1.9 %shard_map.117 = (bf16[2,256,256]{2,1,0:T(8,128)(2,1)S(1)}, bf16[2,256,256]{2,1,0:T(8,128)(2,1)S(1)}) custom-call(bf16[2,128,256]{2,1,0:T(8,128)(2,1)S(1)} %get-tuple-element.34.refs_0_, bf16[2,2,128,256]{3,2,1,0:T(8,128)(2,1)S(1)} %collective-permute-done.24.refs_1_, bf16[2,128,256]{2,1,0:T(8,128)(2,1)S(1)} %collective-permute-done.25.refs_2_, ...), custom_call_target="tpu_custom_call" | custom-call | flops 536870912 | bytes 2883584 | tf_op jit(solution)/shard_map/pallas_call | solution.py:80
  85.0 0.7 collective-permute-start.32
  85.7 4.5 %shard_map.115 = bf16[2048,256]{1,0:T(8,128)(2,1)} custom-call(f32[8,256,256]{2,1,0:T(8,128)S(1)} %copy-done.1, bf16[10,256,256]{2,1,0:T(8,128)(2,1)S(1)} %get-tuple-element.19.mine_ref, bf16[10,256,256]{2,1,0:T(8,128)(2,1)S(1)} %collective-permute-done.13.theirs_ref, bf16[3,256,256]{2,1,0:T(8,128)(2,1)S(1)} %copy-done.2, ...), custom_call_target="tpu_custom_call" | custom-call | flops 1879048192 | bytes 6291456 | tf_op jit(solution)/shard_map/pallas_call | solution.py:166
  90.2 0.6 collective-permute-done.23.refs_3_
  90.8 5.0 %collective-permute-done.32.refs_2_ = bf16[2,256,256]{2,1,0:T(8,128)(2,1)S(1)} collective-permute-done((bf16[2,256,256]{2,1,0:T(8,128)(2,1)S(1)}, bf16[2,256,256]{2,1,0:T(8,128)(2,1)S(1)}, u32[]{:S(2)}, u32[]{:S(2)}) %collective-permute-start.32) | collective-permute-done | bytes 262176 | tf_op jit(solution)/shard_map/ppermute | solution.py:223
  95.8 2.0 %shard_map.118 = bf16[2048,256]{1,0:T(8,128)(2,1)} custom-call(s32[1]{0:T(128)} %bitcast.group_ref, bf16[2,256,256]{2,1,0:T(8,128)(2,1)S(1)} %get-tuple-element.24.refs_0_, bf16[2,256,256]{2,1,0:T(8,128)(2,1)S(1)} %get-tuple-element.25.refs_1_, bf16[2,256,256]{2,1,0:T(8,128)(2,1)S(1)} %collective-permute-done.32.refs_2_, ...), custom_call_target="tpu_custom_call" | custom-call | bytes 2097152 | tf_op jit(solution)/shard_map/pallas_call | solution.py:208
  (90 shorter events, 1.8 us)
Async XLA Ops:
  2.2 5.2 %copy-start.11 = (s32[8]{0:T(128)S(1)}, s32[8]{0:T(128)}, u32[]{:S(2)}) copy-start(s32[8]{0:T(128)} %param.15) | copy-start | bytes 100
  2.3 2.1 %collective-permute-start = (bf16[8,128,256]{2,1,0:T(8,128)(2,1)S(1)}, bf16[8,128,256]{2,1,0:T(8,128)(2,1)S(1)}, u32[]{:S(2)}, u32[]{:S(2)}) collective-permute-start(bf16[8,128,256]{2,1,0:T(8,128)(2,1)S(1)} %pad_maximum_fusion), channel_id=1, source_target_pairs={{0,1},{1,0},{2,3},{3,2},{4,5},{5,4},{6,7},{7,6},{8,9},{9,8},{10,11... | collective-permute-start | bytes 1572872 | tf_op jit(solution)/shard_map/ppermute | solution.py:223
  4.3 14.0 %copy-start.7 = (bf16[256,512]{1,0:T(8,128)(2,1)S(1)}, bf16[256,512]{1,0:T(8,128)(2,1)}, u32[]{:S(2)}) copy-start(bf16[256,512]{1,0:T(8,128)(2,1)} %param.10) | copy-start | bytes 786436
  4.4 14.0 %copy-start.9 = (bf16[8,8,256]{2,1,0:T(8,128)(2,1)S(1)}, bf16[8,8,256]{2,1,0:T(8,128)(2,1)}, u32[]{:S(2)}) copy-start(bf16[8,8,256]{2,1,0:T(8,128)(2,1)} %param.13) | copy-start | bytes 98308
  4.4 14.0 %copy-start.10 = (bf16[8,2,256]{2,1,0:T(2,128)(2,1)S(1)}, bf16[8,2,256]{2,1,0:T(2,128)(2,1)}, u32[]{:S(2)}) copy-start(bf16[8,2,256]{2,1,0:T(2,128)(2,1)} %param.14) | copy-start | bytes 24580
  4.4 10.1 %collective-permute-start.1 = (bf16[2,4,128,256]{3,2,1,0:T(8,128)(2,1)S(1)}, bf16[2,4,128,256]{3,2,1,0:T(8,128)(2,1)S(1)}, u32[]{:S(2)}, u32[]{:S(2)}) collective-permute-start(bf16[2,4,128,256]{3,2,1,0:T(8,128)(2,1)S(1)} %pad_maximum_fusion.1), channel_id=1, source_target_pairs={{0,4},{5,1},{4,8},{9,5},{8,12},{13,9},{12,14},{15,13},{14,10},{11,... | collective-permute-start | bytes 1572872 | tf_op jit(solution)/shard_map/ppermute | solution.py:249
  14.5 17.6 %collective-permute-start.3 = (bf16[2,4,128,256]{3,2,1,0:T(8,128)(2,1)S(1)}, bf16[2,4,128,256]{3,2,1,0:T(8,128)(2,1)S(1)}, u32[]{:S(2)}, u32[]{:S(2)}) collective-permute-start(bf16[2,4,128,256]{3,2,1,0:T(8,128)(2,1)S(1)} %collective-permute-done.1.refs_1_), channel_id=1, source_target_pairs={{0,4},{5,1},{4,8},{9,5},{8,12},{13,9},{12,14},{15,13},{14,10},{11,... | collective-permute-start | bytes 1572872 | tf_op jit(solution)/shard_map/ppermute | solution.py:249
  16.7 12.1 %collective-permute-start.24 = (bf16[2,2,128,256]{3,2,1,0:T(8,128)(2,1)S(1)}, bf16[2,2,128,256]{3,2,1,0:T(8,128)(2,1)S(1)}, u32[]{:S(2)}, u32[]{:S(2)}) collective-permute-start(bf16[2,2,128,256]{3,2,1,0:T(8,128)(2,1)S(1)} %pad_maximum_fusion.3), channel_id=1, source_target_pairs={{0,4},{5,1},{4,8},{9,5},{8,12},{13,9},{12,14},{15,13},{14,10},{11,... | collective-permute-start | bytes 786440 | tf_op jit(solution)/shard_map/ppermute | solution.py:249
  19.2 20.1 %all-to-all-start = ((bf16[8,40,512]{2,1,0:T(8,128)(2,1)}), bf16[8,40,512]{2,1,0:T(8,128)(2,1)S(1)}, u32[]{:S(2)}, u32[]{:S(2)}) async-start(bf16[8,40,512]{2,1,0:T(8,128)(2,1)} %maximum_maximum_fusion), calls=%async_computation | async-start | bytes 655360 | tf_op jit(solution)/shard_map/all_to_all | solution.py:315
  28.8 8.1 %collective-permute-start.26 = (bf16[2,2,128,256]{3,2,1,0:T(8,128)(2,1)S(1)}, bf16[2,2,128,256]{3,2,1,0:T(8,128)(2,1)S(1)}, u32[]{:S(2)}, u32[]{:S(2)}) collective-permute-start(bf16[2,2,128,256]{3,2,1,0:T(8,128)(2,1)S(1)} %collective-permute-done.24.refs_1_), channel_id=1, source_target_pairs={{0,4},{5,1},{4,8},{9,5},{8,12},{13,9},{12,14},{15,13},{14,10},{11,... | collective-permute-start | bytes 786440 | tf_op jit(solution)/shard_map/ppermute | solution.py:249
  32.1 10.0 %collective-permute-start.5 = (bf16[2,4,128,256]{3,2,1,0:T(8,128)(2,1)S(1)}, bf16[2,4,128,256]{3,2,1,0:T(8,128)(2,1)S(1)}, u32[]{:S(2)}, u32[]{:S(2)}) collective-permute-start(bf16[2,4,128,256]{3,2,1,0:T(8,128)(2,1)S(1)} %collective-permute-done.3.refs_3_), channel_id=1, source_target_pairs={{0,4},{5,1},{4,8},{9,5},{8,12},{13,9},{12,14},{15,13},{14,10},{11,... | collective-permute-start | bytes 1572872 | tf_op jit(solution)/shard_map/ppermute | solution.py:249
  36.8 12.7 %collective-permute-start.2 = (bf16[4,128,256]{2,1,0:T(8,128)(2,1)}, bf16[4,128,256]{2,1,0:T(8,128)(2,1)S(1)}, u32[]{:S(2)}, u32[]{:S(2)}) collective-permute-start(bf16[4,128,256]{2,1,0:T(8,128)(2,1)} %slice_bitcast_fusion.2), channel_id=1, source_target_pairs={{0,1},{1,0},{2,3},{3,2},{4,5},{5,4},{6,7},{7,6},{8,9},{9,8},{10,11... | collective-permute-start | bytes 786440 | tf_op jit(solution)/shard_map/ppermute | solution.py:223
  36.8 12.1 %collective-permute-start.28 = (bf16[2,2,128,256]{3,2,1,0:T(8,128)(2,1)S(1)}, bf16[2,2,128,256]{3,2,1,0:T(8,128)(2,1)S(1)}, u32[]{:S(2)}, u32[]{:S(2)}) collective-permute-start(bf16[2,2,128,256]{3,2,1,0:T(8,128)(2,1)S(1)} %collective-permute-done.26.refs_3_), channel_id=1, source_target_pairs={{0,4},{5,1},{4,8},{9,5},{8,12},{13,9},{12,14},{15,13},{14,10},{11,... | collective-permute-start | bytes 786440 | tf_op jit(solution)/shard_map/ppermute | solution.py:249
  39.5 10.1 %copy-start.8 = (bf16[2,128,256]{2,1,0:T(8,128)(2,1)S(1)}, bf16[2,128,256]{2,1,0:T(8,128)(2,1)}, u32[]{:S(2)}) copy-start(bf16[2,128,256]{2,1,0:T(8,128)(2,1)} %slice_bitcast_fusion.6) | copy-start | bytes 393220
  39.5 13.1 %copy-start.6 = (bf16[2,2,128,256]{3,2,1,0:T(8,128)(2,1)S(1)}, bf16[2,2,128,256]{3,2,1,0:T(8,128)(2,1)}, u32[]{:S(2)}) copy-start(bf16[2,2,128,256]{3,2,1,0:T(8,128)(2,1)} %pad_maximum_fusion.2) | copy-start | bytes 786436
  39.5 6.4 %collective-permute-start.10 = (bf16[256,512]{1,0:T(8,128)(2,1)S(1)}, bf16[256,512]{1,0:T(8,128)(2,1)S(1)}, u32[]{:S(2)}, u32[]{:S(2)}) collective-permute-start(bf16[256,512]{1,0:T(8,128)(2,1)S(1)} %fusion.3.refs_9_), channel_id=1, source_target_pairs={{0,16},{16,0},{1,17},{17,1},{2,18},{18,2},{3,19},{19,3},{4,20},{20... | collective-permute-start | bytes 786440 | tf_op jit(solution)/shard_map/ppermute | solution.py:223
  42.2 6.7 %collective-permute-start.7 = (bf16[2,2,128,256]{3,2,1,0:T(8,128)(2,1)S(1)}, bf16[2,2,128,256]{3,2,1,0:T(8,128)(2,1)S(1)}, u32[]{:S(2)}, u32[]{:S(2)}) collective-permute-start(bf16[2,2,128,256]{3,2,1,0:T(8,128)(2,1)S(1)} %constant_dynamic-slice_fusion.2), channel_id=1, source_target_pairs={{0,4},{5,1},{4,8},{9,5},{8,12},{13,9},{12,14},{15,13},{14,10},{11,... | collective-permute-start | bytes 786440 | tf_op jit(solution)/shard_map/ppermute | solution.py:249
  45.0 4.6 %collective-permute-start.4 = (bf16[4,128,256]{2,1,0:T(8,128)(2,1)S(1)}, bf16[4,128,256]{2,1,0:T(8,128)(2,1)S(1)}, u32[]{:S(2)}, u32[]{:S(2)}) collective-permute-start(bf16[4,128,256]{2,1,0:T(8,128)(2,1)S(1)} %slice_bitcast_fusion.1), channel_id=1, source_target_pairs={{0,1},{1,0},{2,3},{3,2},{4,5},{5,4},{6,7},{7,6},{8,9},{9,8},{10,11... | collective-permute-start | bytes 786440 | tf_op jit(solution)/shard_map/ppermute | solution.py:223
  46.0 4.2 %collective-permute-start.9 = (bf16[256,512]{1,0:T(8,128)(2,1)S(1)}, bf16[256,512]{1,0:T(8,128)(2,1)S(1)}, u32[]{:S(2)}, u32[]{:S(2)}) collective-permute-start(bf16[256,512]{1,0:T(8,128)(2,1)S(1)} %fusion.3.refs_9_), channel_id=1, source_target_pairs={{0,1},{1,0},{2,3},{3,2},{4,5},{5,4},{6,7},{7,6},{8,9},{9,8},{10,11... | collective-permute-start | bytes 786440 | tf_op jit(solution)/shard_map/ppermute | solution.py:223
  48.9 3.7 %collective-permute-start.11 = (bf16[256,512]{1,0:T(8,128)(2,1)S(1)}, bf16[256,512]{1,0:T(8,128)(2,1)S(1)}, u32[]{:S(2)}, u32[]{:S(2)}) collective-permute-start(bf16[256,512]{1,0:T(8,128)(2,1)S(1)} %collective-permute-done.10.refs_11_), channel_id=1, source_target_pairs={{0,1},{1,0},{2,3},{3,2},{4,5},{5,4},{6,7},{7,6},{8,9},{9,8},{10,11... | collective-permute-start | bytes 786440 | tf_op jit(solution)/shard_map/ppermute | solution.py:223
  48.9 6.2 %collective-permute-start.6 = (bf16[4,128,256]{2,1,0:T(8,128)(2,1)S(1)}, bf16[4,128,256]{2,1,0:T(8,128)(2,1)S(1)}, u32[]{:S(2)}, u32[]{:S(2)}) collective-permute-start(bf16[4,128,256]{2,1,0:T(8,128)(2,1)S(1)} %slice_bitcast_fusion), channel_id=1, source_target_pairs={{0,1},{1,0},{2,3},{3,2},{4,5},{5,4},{6,7},{7,6},{8,9},{9,8},{10,11... | collective-permute-start | bytes 786440 | tf_op jit(solution)/shard_map/ppermute | solution.py:223
  49.5 5.6 %collective-permute-start.8 = (bf16[2,128,256]{2,1,0:T(8,128)(2,1)S(1)}, bf16[2,128,256]{2,1,0:T(8,128)(2,1)S(1)}, u32[]{:S(2)}, u32[]{:S(2)}) collective-permute-start(bf16[2,128,256]{2,1,0:T(8,128)(2,1)S(1)} %slice_bitcast_fusion.12), channel_id=1, source_target_pairs={{0,1},{1,0},{2,3},{3,2},{4,5},{5,4},{6,7},{7,6},{8,9},{9,8},{10,11... | collective-permute-start | bytes 393224 | tf_op jit(solution)/shard_map/ppermute | solution.py:223
  49.7 24.7 %collective-permute-start.25 = (bf16[2,128,256]{2,1,0:T(8,128)(2,1)S(1)}, bf16[2,128,256]{2,1,0:T(8,128)(2,1)S(1)}, u32[]{:S(2)}, u32[]{:S(2)}) collective-permute-start(bf16[2,128,256]{2,1,0:T(8,128)(2,1)S(1)} %copy-done.8), channel_id=1, source_target_pairs={{0,1},{1,0},{2,3},{3,2},{4,5},{5,4},{6,7},{7,6},{8,9},{9,8},{10,11... | collective-permute-start | bytes 393224 | tf_op jit(solution)/shard_map/ppermute | solution.py:223
  50.2 26.8 %collective-permute-start.30 = (bf16[2,1,128,256]{3,2,1,0:T(8,128)(2,1)S(1)}, bf16[2,1,128,256]{3,2,1,0:T(8,128)(2,1)S(1)}, u32[]{:S(2)}, u32[]{:S(2)}) collective-permute-start(bf16[2,1,128,256]{3,2,1,0:T(8,128)(2,1)S(1)} %constant_dynamic-slice_fusion), channel_id=1, source_target_pairs={{0,4},{5,1},{4,8},{9,5},{8,12},{13,9},{12,14},{15,13},{14,10},{11,... | collective-permute-start | bytes 393224 | tf_op jit(solution)/shard_map/ppermute | solution.py:249
  52.7 6.4 %collective-permute-start.15 = (bf16[2,2,128,256]{3,2,1,0:T(8,128)(2,1)S(1)}, bf16[2,2,128,256]{3,2,1,0:T(8,128)(2,1)S(1)}, u32[]{:S(2)}, u32[]{:S(2)}) collective-permute-start(bf16[2,2,128,256]{3,2,1,0:T(8,128)(2,1)S(1)} %copy-done.6), channel_id=1, source_target_pairs={{0,4},{5,1},{4,8},{9,5},{8,12},{13,9},{12,14},{15,13},{14,10},{11,... | collective-permute-start | bytes 786440 | tf_op jit(solution)/shard_map/ppermute | solution.py:249
  57.4 11.6 %copy-start = (f32[256]{0:T(256)S(1)}, f32[256]{0:T(256)}, u32[]{:S(2)}) copy-start(f32[256]{0:T(256)} %param.12) | copy-start | bytes 3076
  57.4 11.6 %collective-permute-start.12 = (bf16[4,256,256]{2,1,0:T(8,128)(2,1)S(1)}, bf16[4,256,256]{2,1,0:T(8,128)(2,1)S(1)}, u32[]{:S(2)}, u32[]{:S(2)}) collective-permute-start(bf16[4,256,256]{2,1,0:T(8,128)(2,1)S(1)} %get-tuple-element.17), channel_id=1, source_target_pairs={{0,16},{16,0},{1,17},{17,1},{2,18},{18,2},{3,19},{19,3},{4,20},{20... | collective-permute-start | bytes 1572872 | tf_op jit(solution)/shard_map/ppermute | solution.py:223
  59.1 6.4 %collective-permute-start.17 = (bf16[2,2,128,256]{3,2,1,0:T(8,128)(2,1)S(1)}, bf16[2,2,128,256]{3,2,1,0:T(8,128)(2,1)S(1)}, u32[]{:S(2)}, u32[]{:S(2)}) collective-permute-start(bf16[2,2,128,256]{3,2,1,0:T(8,128)(2,1)S(1)} %collective-permute-done.15.refs_1_), channel_id=1, source_target_pairs={{0,4},{5,1},{4,8},{9,5},{8,12},{13,9},{12,14},{15,13},{14,10},{11,... | collective-permute-start | bytes 786440 | tf_op jit(solution)/shard_map/ppermute | solution.py:249
  65.5 6.4 %collective-permute-start.19 = (bf16[2,2,128,256]{3,2,1,0:T(8,128)(2,1)S(1)}, bf16[2,2,128,256]{3,2,1,0:T(8,128)(2,1)S(1)}, u32[]{:S(2)}, u32[]{:S(2)}) collective-permute-start(bf16[2,2,128,256]{3,2,1,0:T(8,128)(2,1)S(1)} %collective-permute-done.17.refs_3_), channel_id=1, source_target_pairs={{0,4},{5,1},{4,8},{9,5},{8,12},{13,9},{12,14},{15,13},{14,10},{11,... | collective-permute-start | bytes 786440 | tf_op jit(solution)/shard_map/ppermute | solution.py:249
  69.0 7.9 %copy-start.2 = (bf16[3,256,256]{2,1,0:T(8,128)(2,1)S(1)}, bf16[3,256,256]{2,1,0:T(8,128)(2,1)}, u32[]{:S(2)}) copy-start(bf16[3,256,256]{2,1,0:T(8,128)(2,1)} %res_mine_ref.1) | copy-start | bytes 1179652
  70.8 14.9 %collective-permute-start.13 = (bf16[10,256,256]{2,1,0:T(8,128)(2,1)S(1)}, bf16[10,256,256]{2,1,0:T(8,128)(2,1)S(1)}, u32[]{:S(2)}, u32[]{:S(2)}) collective-permute-start(bf16[10,256,256]{2,1,0:T(8,128)(2,1)S(1)} %get-tuple-element.19.mine_ref), channel_id=1, source_target_pairs={{0,1},{1,0},{2,3},{3,2},{4,5},{5,4},{6,7},{7,6},{8,9},{9,8},{10,11... | collective-permute-start | bytes 3932168 | tf_op jit(solution)/shard_map/ppermute | solution.py:223
  70.8 6.7 %collective-permute-start.16 = (bf16[2,128,256]{2,1,0:T(8,128)(2,1)S(1)}, bf16[2,128,256]{2,1,0:T(8,128)(2,1)S(1)}, u32[]{:S(2)}, u32[]{:S(2)}) collective-permute-start(bf16[2,128,256]{2,1,0:T(8,128)(2,1)S(1)} %slice_bitcast_fusion.10), channel_id=1, source_target_pairs={{0,1},{1,0},{2,3},{3,2},{4,5},{5,4},{6,7},{7,6},{8,9},{9,8},{10,11... | collective-permute-start | bytes 393224 | tf_op jit(solution)/shard_map/ppermute | solution.py:223
  71.9 5.0 %collective-permute-start.21 = (bf16[2,1,128,256]{3,2,1,0:T(8,128)(2,1)S(1)}, bf16[2,1,128,256]{3,2,1,0:T(8,128)(2,1)S(1)}, u32[]{:S(2)}, u32[]{:S(2)}) collective-permute-start(bf16[2,1,128,256]{3,2,1,0:T(8,128)(2,1)S(1)} %constant_dynamic-slice_fusion.1), channel_id=1, source_target_pairs={{0,4},{5,1},{4,8},{9,5},{8,12},{13,9},{12,14},{15,13},{14,10},{11,... | collective-permute-start | bytes 393224 | tf_op jit(solution)/shard_map/ppermute | solution.py:249
  74.3 3.3 %collective-permute-start.18 = (bf16[2,128,256]{2,1,0:T(8,128)(2,1)S(1)}, bf16[2,128,256]{2,1,0:T(8,128)(2,1)S(1)}, u32[]{:S(2)}, u32[]{:S(2)}) collective-permute-start(bf16[2,128,256]{2,1,0:T(8,128)(2,1)S(1)} %slice_bitcast_fusion.9), channel_id=1, source_target_pairs={{0,1},{1,0},{2,3},{3,2},{4,5},{5,4},{6,7},{7,6},{8,9},{9,8},{10,11... | collective-permute-start | bytes 393224 | tf_op jit(solution)/shard_map/ppermute | solution.py:223
  76.9 1.3 %collective-permute-start.20 = (bf16[2,128,256]{2,1,0:T(8,128)(2,1)S(1)}, bf16[2,128,256]{2,1,0:T(8,128)(2,1)S(1)}, u32[]{:S(2)}, u32[]{:S(2)}) collective-permute-start(bf16[2,128,256]{2,1,0:T(8,128)(2,1)S(1)} %slice_bitcast_fusion.8), channel_id=1, source_target_pairs={{0,1},{1,0},{2,3},{3,2},{4,5},{5,4},{6,7},{7,6},{8,9},{9,8},{10,11... | collective-permute-start | bytes 393224 | tf_op jit(solution)/shard_map/ppermute | solution.py:223
  77.0 8.7 %collective-permute-start.14 = (bf16[3,256,256]{2,1,0:T(8,128)(2,1)S(1)}, bf16[3,256,256]{2,1,0:T(8,128)(2,1)S(1)}, u32[]{:S(2)}, u32[]{:S(2)}) collective-permute-start(bf16[3,256,256]{2,1,0:T(8,128)(2,1)S(1)} %copy-done.2), channel_id=1, source_target_pairs={{0,1},{1,0},{2,3},{3,2},{4,5},{5,4},{6,7},{7,6},{8,9},{9,8},{10,11... | collective-permute-start | bytes 1179656 | tf_op jit(solution)/shard_map/ppermute | solution.py:223
  77.5 4.1 %collective-permute-start.27 = (bf16[2,128,256]{2,1,0:T(8,128)(2,1)S(1)}, bf16[2,128,256]{2,1,0:T(8,128)(2,1)S(1)}, u32[]{:S(2)}, u32[]{:S(2)}) collective-permute-start(bf16[2,128,256]{2,1,0:T(8,128)(2,1)S(1)} %slice_bitcast_fusion.5), channel_id=1, source_target_pairs={{0,1},{1,0},{2,3},{3,2},{4,5},{5,4},{6,7},{7,6},{8,9},{9,8},{10,11... | collective-permute-start | bytes 393224 | tf_op jit(solution)/shard_map/ppermute | solution.py:223
  77.6 5.5 %collective-permute-start.29 = (bf16[2,128,256]{2,1,0:T(8,128)(2,1)S(1)}, bf16[2,128,256]{2,1,0:T(8,128)(2,1)S(1)}, u32[]{:S(2)}, u32[]{:S(2)}) collective-permute-start(bf16[2,128,256]{2,1,0:T(8,128)(2,1)S(1)} %slice_bitcast_fusion.4), channel_id=1, source_target_pairs={{0,1},{1,0},{2,3},{3,2},{4,5},{5,4},{6,7},{7,6},{8,9},{9,8},{10,11... | collective-permute-start | bytes 393224 | tf_op jit(solution)/shard_map/ppermute | solution.py:223
  78.3 1.3 %collective-permute-start.22 = (bf16[1,128,256]{2,1,0:T(8,128)(2,1)S(1)}, bf16[1,128,256]{2,1,0:T(8,128)(2,1)S(1)}, u32[]{:S(2)}, u32[]{:S(2)}) collective-permute-start(bf16[1,128,256]{2,1,0:T(8,128)(2,1)S(1)} %slice_bitcast_fusion.14), channel_id=1, source_target_pairs={{0,1},{1,0},{2,3},{3,2},{4,5},{5,4},{6,7},{7,6},{8,9},{9,8},{10,11... | collective-permute-start | bytes 196616 | tf_op jit(solution)/shard_map/ppermute | solution.py:223
  79.5 3.6 %collective-permute-start.31 = (bf16[1,128,256]{2,1,0:T(8,128)(2,1)S(1)}, bf16[1,128,256]{2,1,0:T(8,128)(2,1)S(1)}, u32[]{:S(2)}, u32[]{:S(2)}) collective-permute-start(bf16[1,128,256]{2,1,0:T(8,128)(2,1)S(1)} %slice_bitcast_fusion.13), channel_id=1, source_target_pairs={{0,1},{1,0},{2,3},{3,2},{4,5},{5,4},{6,7},{7,6},{8,9},{9,8},{10,11... | collective-permute-start | bytes 196616 | tf_op jit(solution)/shard_map/ppermute | solution.py:223
  81.6 4.1 %copy-start.1 = (f32[8,256,256]{2,1,0:T(8,128)S(1)}, f32[8,256,256]{2,1,0:T(8,128)}, u32[]{:S(2)}) copy-start(f32[8,256,256]{2,1,0:T(8,128)} %get-tuple-element.18.up_ref) | copy-start | bytes 6291460
  81.6 4.1 %copy-start.3 = (bf16[256,256]{1,0:T(8,128)(2,1)S(1)}, bf16[256,256]{1,0:T(8,128)(2,1)}, u32[]{:S(2)}) copy-start(bf16[256,256]{1,0:T(8,128)(2,1)} %skip_ref.1) | copy-start | bytes 393220
  81.6 4.1 %copy-start.4 = (f32[256]{0:T(256)S(1)}, f32[256]{0:T(256)}, u32[]{:S(2)}) copy-start(f32[256]{0:T(256)} %param.17) | copy-start | bytes 3076
  81.6 4.1 %copy-start.5 = (f32[256]{0:T(256)S(1)}, f32[256]{0:T(256)}, u32[]{:S(2)}) copy-start(f32[256]{0:T(256)} %param.19) | copy-start | bytes 3076
  81.6 9.2 %collective-permute-start.23 = (bf16[2,256,256]{2,1,0:T(8,128)(2,1)S(1)}, bf16[2,256,256]{2,1,0:T(8,128)(2,1)S(1)}, u32[]{:S(2)}, u32[]{:S(2)}) collective-permute-start(bf16[2,256,256]{2,1,0:T(8,128)(2,1)S(1)} %get-tuple-element.22), channel_id=1, source_target_pairs={{0,16},{16,0},{1,17},{17,1},{2,18},{18,2},{3,19},{19,3},{4,20},{20... | collective-permute-start | bytes 786440 | tf_op jit(solution)/shard_map/ppermute | solution.py:223
  85.0 10.8 %collective-permute-start.32 = (bf16[2,256,256]{2,1,0:T(8,128)(2,1)S(1)}, bf16[2,256,256]{2,1,0:T(8,128)(2,1)S(1)}, u32[]{:S(2)}, u32[]{:S(2)}) collective-permute-start(bf16[2,256,256]{2,1,0:T(8,128)(2,1)S(1)} %get-tuple-element.26), channel_id=1, source_target_pairs={{0,16},{16,0},{1,17},{17,1},{2,18},{18,2},{3,19},{19,3},{4,20},{20... | collective-permute-start | bytes 786440 | tf_op jit(solution)/shard_map/ppermute | solution.py:223

commit v2 on v1

--- a/solution.py
+++ b/solution.py
@@ -47,7 +47,7 @@
             stream = ring_stream(
                 lax.rem(place + (2 * taker - 1) * distance + count, count), count
             )
-            source = block if len(block.shape) == 3 else block.at[0]
+            source = block if len(block.shape) == 3 else block.at[passed]
             part = source.shape[0]
             first = 0 if part == taps else taker * part
             target = kernel_rows.at[
@@ -91,11 +91,6 @@
             pltpu.SemaphoreType.DMA((len(blocks),)),
         ],
         compiler_params=pltpu.CompilerParams(vmem_limit_bytes=VMEM_LIMIT),
-        cost_estimate=pl.CostEstimate(
-            flops=4 * taps * sessions * depth * width,
-            bytes_accessed=2 * taps * depth * width + 4 * sessions * depth + 6 * taps * sessions * width,
-            transcendentals=0,
-        ),
     )(*blocks, *sides)
 
 
@@ -126,11 +121,6 @@
         in_specs=[pl.BlockSpec(memory_space=pltpu.SMEM), VMEM, VMEM, VMEM, VMEM],
         out_specs=(VMEM, VMEM),
         compiler_params=pltpu.CompilerParams(vmem_limit_bytes=VMEM_LIMIT),
-        cost_estimate=pl.CostEstimate(
-            flops=20 * taps * sessions * width,
-            bytes_accessed=40 * taps * sessions * width,
-            transcendentals=2 * taps * sessions * width,
-        ),
     )(group, own, other, prev, bias)
 
 
@@ -172,16 +162,12 @@
         out_specs=pl.BlockSpec((block * steps, width), lambda i: (i, 0)),
         scratch_shapes=[pltpu.VMEM((width // 128, block * steps, 128), F32)],
         compiler_params=pltpu.CompilerParams(vmem_limit_bytes=VMEM_LIMIT),
-        cost_estimate=pl.CostEstimate(
-            flops=2 * up.size * (2 * res_mine.shape[0] + 1) * res_mine.shape[2],
-            bytes_accessed=12 * up.size,
-            transcendentals=up.size,
-        ),
     )(up, mine, theirs, res_mine, res_theirs, res_bias, skip_weight, skip_bias)
 
 
 def weave_kernel(group_ref, *refs):
-    owns, others, (out_ref, frames) = refs[: len(refs) // 2 - 1], refs[len(refs) // 2 - 1 : -2], refs[-2:]
+    owns, others = refs[: len(refs) // 2 - 1], refs[len(refs) // 2 - 1 : -2]
+    out_ref, frames = refs[-2:]
     group = group_ref[0]
     block, width = owns[0].shape[1:]
     steps = frames.shape[1] // block
@@ -213,9 +199,6 @@
         out_specs=pl.BlockSpec((block * steps, width), lambda i: (i, 0)),
         scratch_shapes=[pltpu.VMEM((width // 128, block * steps, 128), F32)],
         compiler_params=pltpu.CompilerParams(vmem_limit_bytes=VMEM_LIMIT),
-        cost_estimate=pl.CostEstimate(
-            flops=0, bytes_accessed=4 * sessions * steps * width, transcendentals=0
-        ),
     )(group, *owns, *others)
 
 
@@ -248,7 +231,7 @@
             item = after(item, earlier)
         item = lax.ppermute(item, ("streams", "segment"), self.pairs)
         self.item = item
-        self.blocks += [item, swap(item[1], "segment")]
+        self.blocks += [item, swap(item, "segment")]
         self.steps += [(self.rounds, 0), (self.rounds, 1)]
         return item
 
@@ -283,23 +266,20 @@
         other = swap(own, "segment")
         rings = [Ring(count, own[a:b], other[a:b]) for a, b in cuts]
         up_ring, first_ring, second_ring = rings
-        first_done = up_ring.round()
-        first_ring.round()
-        last = first_done
-        for r in range(2, count // 2 + 1):
-            behind = last
-            last = up_ring.round()
-            first_ring.round()
-            if r >= 3:
-                second_ring.round(behind)
-        while second_ring.rounds < count // 2:
-            second_ring.round()
+        up_seen, first_seen = [], []
+        for r in range(count // 2):
+            up_seen.append(up_ring.round(first_seen[r - 2] if r > 1 else None))
+            first_seen.append(first_ring.round(up_seen[r - 1] if r else None))
+        second_seen = []
+        for r in range(count // 2):
+            second_seen.append(second_ring.round(None if r else up_seen[-2]))
+        first_done, nearly_done = up_seen[0], (first_seen[-2], second_seen[0])
         gathered = [(ring.blocks, ring.steps) for ring in rings]
     else:
         gathered = [
             ([lax.all_gather(own[a:b], "streams", axis=1, tiled=True)], [None]) for a, b in cuts
         ]
-        first_done = own
+        first_done = nearly_done = own
 
     portion = sessions // count
     cap = tail_cache.shape[0] // count
@@ -328,10 +308,11 @@
     res_theirs = swap(res_weight, "segment")
 
     own_up, away_up = spread_taps(sides, *gathered[0], count, F32)
-    other_up = swap(away_up, "groups")
+    other_up = swap(after(away_up, nearly_done), "groups")
     owns, others = [], []
     for blocks, steps in gathered[1:]:
         own_tail, away_tail = spread_taps(sides, blocks, steps, count, BF16)
+        own_up = after(own_up, away_tail)
         owns.append(own_tail)
         others.append(swap(away_tail, "groups"))
 

time: 98.1 us -> 101 us (1.030)
  local copies, waits for them, and re-layouts: 3.35 us -> 9.16 us
  starting transfers between devices: 43.9 us -> 39.7 us
  Pallas kernels: 14.3 us -> 16.7 us
  waiting for transfers between devices: 32.8 us -> 30.9 us
    ppermute x12, starting transfers between devices: 30.9 us -> 26.6 us  [round(): item = lax.ppermute(item, ('streams', 'segment'), self.pairs)]
    ppermute x12, waiting for transfers between devices: 22.3 us -> 18.3 us  [round(): item = lax.ppermute(item, ('streams', 'segment'), self.pairs)]
    unnamed x29 -> x35, local copies, waits for them, and re-layouts: 0.15 us -> 3.57 us
    pallas_call x3, Pallas kernels: 5.99 us -> 8.46 us  [spread_taps(): pl.pallas_call(functools.partial(spread_kernel, count, steps), out_shape=...]
    ppermute x21, waiting for transfers between devices: 10.5 us -> 12.6 us  [swap(): return lax.ppermute(value, axis, [(0, 1), (1, 0)])]
    squeeze x12 -> x0, local copies, waits for them, and re-layouts: 1.48 us -> none  [round(): self.blocks += [item, swap(item[1], 'segment')]]
    all_to_all x1, starting transfers between devices: 3.78 us -> 4.79 us  [local(): lax.all_to_all(parcel, 'streams', split_axis=0, concat_axis=0, tiled=True)]
  transfers between devices with their start and end apart: 34 -> 34, of which waited for: 14 -> 12; matrix products, arithmetic and copies ran while one was open for 4% -> 7% of each run, Pallas kernels for 12% -> 13%
where the time goes in v2:
time: 101 us
  starting transfers between devices  39.7 us (39%)
  waiting for transfers between devices  30.9 us (31%)
  Pallas kernels  16.7 us (17%)
  local copies, waits for them, and re-layouts  9.16 us (9%)
  other arithmetic  2.83 us (3%)
    ppermute x12, starting transfers between devices, round(): item = lax.ppermute(item, ('streams', 'segment'), self.pairs)  26.6 us
    ppermute x12, waiting for transfers between devices, round(): item = lax.ppermute(item, ('streams', 'segment'), self.pairs)  18.3 us
    ppermute x21, waiting for transfers between devices, swap(): return lax.ppermute(value, axis, [(0, 1), (1, 0)])  12.6 us
    pallas_call x3, Pallas kernels, spread_taps(): pl.pallas_call(functools.partial(spread_kernel, count, steps), out_shape=...  8.46 us
    ppermute x21, starting transfers between devices, swap(): return lax.ppermute(value, axis, [(0, 1), (1, 0)])  8.33 us
    all_to_all x1, starting transfers between devices, local(): lax.all_to_all(parcel, 'streams', split_axis=0, concat_axis=0, tiled=True)  4.79 us
    pallas_call x1, Pallas kernels, residual(): pl.pallas_call(residual_kernel, out_shape=jax.ShapeDtypeStruct((sessions...  4.44 us
    unnamed x35, local copies, waits for them, and re-layouts  3.57 us
  transfers between devices with their start and end apart: 34, of which 12 were waited for; matrix products, arithmetic and copies ran while one was open for 7% of the time, Pallas kernels for 13%

profile of v2, /device:TPU:0, one launch (start us, length us, event | category | flops | bytes accessed | tf_op | source)
XLA Modules:
  0.0 100.9 jit_solution(17756379168884261811)
XLA Ops:
  0.6 1.5 %constant_dynamic-slice_fusion.3 = (bf16[128,4,256]{2,1,0:T(4,128)(2,1)S(1)}, bf16[128,4,256]{2,1,0:T(4,128)(2,1)S(1)}) fusion(bf16[128,16,256]{2,1,0:T(8,128)(2,1)} %param.11, s32[]{:T(128)S(6)} %select_n.18, s32[]{:T(128)S(6)} %select_n.17), kind=kLoop, calls=%fused_computation.29 | loop fusion | bytes 1048584 | tf_op jit(solution)/shard_map/dynamic_slice | solution.py:260
  2.3 0.5 collective-permute-start
  2.8 1.5 %collective-permute-done = bf16[8,128,256]{2,1,0:T(8,128)(2,1)S(1)} collective-permute-done((bf16[8,128,256]{2,1,0:T(8,128)(2,1)S(1)}, bf16[8,128,256]{2,1,0:T(8,128)(2,1)S(1)}, u32[]{:S(2)}, u32[]{:S(2)}) %collective-permute-start) | collective-permute-done | bytes 524320 | tf_op jit(solution)/shard_map/ppermute | solution.py:206
  4.4 3.0 %collective-permute-start.1 = (bf16[2,4,128,256]{3,2,1,0:T(8,128)(2,1)S(1)}, bf16[2,4,128,256]{3,2,1,0:T(8,128)(2,1)S(1)}, u32[]{:S(2)}, u32[]{:S(2)}) collective-permute-start(bf16[2,4,128,256]{3,2,1,0:T(8,128)(2,1)S(1)} %pad_maximum_fusion.1), channel_id=1, source_target_pairs={{0,4},{5,1},{4,8},{9,5},{8,12},{13,9},{12,14},{15,13},{14,10},{11,... | collective-permute-start | bytes 1572872 | tf_op jit(solution)/shard_map/ppermute | solution.py:232
  7.6 0.8 maximum_maximum_fusion
  8.4 6.1 %collective-permute-done.1.refs_1_ = bf16[2,4,128,256]{3,2,1,0:T(8,128)(2,1)S(1)} collective-permute-done((bf16[2,4,128,256]{3,2,1,0:T(8,128)(2,1)S(1)}, bf16[2,4,128,256]{3,2,1,0:T(8,128)(2,1)S(1)}, u32[]{:S(2)}, u32[]{:S(2)}) %collective-permute-start.1) | collective-permute-done | bytes 524320 | tf_op jit(solution)/shard_map/ppermute | solution.py:232
  14.5 2.1 %collective-permute-start.3 = (bf16[2,4,128,256]{3,2,1,0:T(8,128)(2,1)S(1)}, bf16[2,4,128,256]{3,2,1,0:T(8,128)(2,1)S(1)}, u32[]{:S(2)}, u32[]{:S(2)}) collective-permute-start(bf16[2,4,128,256]{3,2,1,0:T(8,128)(2,1)S(1)} %collective-permute-done.1.refs_1_), channel_id=1, source_target_pairs={{0,4},{5,1},{4,8},{9,5},{8,12},{13,9},{12,14},{15,13},{14,10},{11,... | collective-permute-start | bytes 1572872 | tf_op jit(solution)/shard_map/ppermute | solution.py:232
  16.6 0.7 slice_bitcast_fusion.1
  17.3 4.8 %all-to-all-start = ((bf16[8,40,512]{2,1,0:T(8,128)(2,1)}), bf16[8,40,512]{2,1,0:T(8,128)(2,1)}, u32[]{:S(2)}, u32[]{:S(2)}) async-start(bf16[8,40,512]{2,1,0:T(8,128)(2,1)} %maximum_maximum_fusion), calls=%async_computation | async-start | bytes 655360 | tf_op jit(solution)/shard_map/all_to_all | solution.py:295
  22.1 2.1 %collective-permute-start.5 = (bf16[2,2,128,256]{3,2,1,0:T(8,128)(2,1)S(1)}, bf16[2,2,128,256]{3,2,1,0:T(8,128)(2,1)S(1)}, u32[]{:S(2)}, u32[]{:S(2)}) collective-permute-start(bf16[2,2,128,256]{3,2,1,0:T(8,128)(2,1)S(1)} %pad_maximum_fusion.2), channel_id=1, source_target_pairs={{0,4},{5,1},{4,8},{9,5},{8,12},{13,9},{12,14},{15,13},{14,10},{11,... | collective-permute-start | bytes 786440 | tf_op jit(solution)/shard_map/ppermute | solution.py:232
  24.2 7.2 %collective-permute-done.5.refs_1_ = bf16[2,2,128,256]{3,2,1,0:T(8,128)(2,1)S(1)} collective-permute-done((bf16[2,2,128,256]{3,2,1,0:T(8,128)(2,1)S(1)}, bf16[2,2,128,256]{3,2,1,0:T(8,128)(2,1)S(1)}, u32[]{:S(2)}, u32[]{:S(2)}) %collective-permute-start.5) | collective-permute-done | bytes 262176 | tf_op jit(solution)/shard_map/ppermute | solution.py:232
  31.4 3.3 %collective-permute-start.8 = (bf16[2,2,128,256]{3,2,1,0:T(8,128)(2,1)S(1)}, bf16[2,2,128,256]{3,2,1,0:T(8,128)(2,1)}, u32[]{:S(2)}, u32[]{:S(2)}) collective-permute-start(bf16[2,2,128,256]{3,2,1,0:T(8,128)(2,1)S(1)} %collective-permute-done.5.refs_1_), channel_id=1, source_target_pairs={{0,4},{5,1},{4,8},{9,5},{8,12},{13,9},{12,14},{15,13},{14,10},{11,... | collective-permute-start | bytes 786440 | tf_op jit(solution)/shard_map/ppermute | solution.py:232
  34.7 2.5 %collective-permute-start.6 = (bf16[2,4,128,256]{3,2,1,0:T(8,128)(2,1)S(1)}, bf16[2,4,128,256]{3,2,1,0:T(8,128)(2,1)S(1)}, u32[]{:S(2)}, u32[]{:S(2)}) collective-permute-start(bf16[2,4,128,256]{3,2,1,0:T(8,128)(2,1)S(1)} %collective-permute-done.3.refs_3_), channel_id=1, source_target_pairs={{0,4},{5,1},{4,8},{9,5},{8,12},{13,9},{12,14},{15,13},{14,10},{11,... | collective-permute-start | bytes 1572872 | tf_op jit(solution)/shard_map/ppermute | solution.py:232
  37.2 1.4 %collective-permute-done.8.refs_3_ = bf16[2,2,128,256]{3,2,1,0:T(8,128)(2,1)} collective-permute-done((bf16[2,2,128,256]{3,2,1,0:T(8,128)(2,1)S(1)}, bf16[2,2,128,256]{3,2,1,0:T(8,128)(2,1)}, u32[]{:S(2)}, u32[]{:S(2)}) %collective-permute-start.8) | collective-permute-done | bytes 262176 | tf_op jit(solution)/shard_map/ppermute | solution.py:232
  38.6 2.6 %collective-permute-start.16 = (bf16[2,2,128,256]{3,2,1,0:T(8,128)(2,1)}, bf16[2,2,128,256]{3,2,1,0:T(8,128)(2,1)S(1)}, u32[]{:S(2)}, u32[]{:S(2)}) collective-permute-start(bf16[2,2,128,256]{3,2,1,0:T(8,128)(2,1)} %collective-permute-done.8.refs_3_), channel_id=1, source_target_pairs={{0,4},{5,1},{4,8},{9,5},{8,12},{13,9},{12,14},{15,13},{14,10},{11,... | collective-permute-start | bytes 786440 | tf_op jit(solution)/shard_map/ppermute | solution.py:232
  41.2 1.0 slice.48
  42.4 1.6 %pad_maximum_fusion.3 = bf16[2,2,128,256]{3,2,1,0:T(8,128)(2,1)} fusion(bf16[1,2,128,256]{3,2,1,0:T(8,128)(2,1)} %get-tuple-element.44, bf16[1,2,128,256]{3,2,1,0:T(8,128)(2,1)S(1)} %get-tuple-element.46), kind=kLoop, calls=%fused_computation.12 | loop fusion | flops 131072 | bytes 524288 | tf_op jit(solution)/shard_map/stack | solution.py:221
  44.2 2.5 %collective-permute-start.20 = (bf16[2,2,128,256]{3,2,1,0:T(8,128)(2,1)}, bf16[2,2,128,256]{3,2,1,0:T(8,128)(2,1)}, u32[]{:S(2)}, u32[]{:S(2)}) collective-permute-start(bf16[2,2,128,256]{3,2,1,0:T(8,128)(2,1)} %pad_maximum_fusion.3), channel_id=1, source_target_pairs={{0,4},{5,1},{4,8},{9,5},{8,12},{13,9},{12,14},{15,13},{14,10},{11,... | collective-permute-start | bytes 786440 | tf_op jit(solution)/shard_map/ppermute | solution.py:232
  46.7 0.8 copy-done.2
  47.5 1.5 %collective-permute-start.12 = (bf16[256,512]{1,0:T(8,128)(2,1)S(1)}, bf16[256,512]{1,0:T(8,128)(2,1)S(1)}, u32[]{:S(2)}, u32[]{:S(2)}) collective-permute-start(bf16[256,512]{1,0:T(8,128)(2,1)S(1)} %fusion.3.refs_9_), channel_id=1, source_target_pairs={{0,16},{16,0},{1,17},{17,1},{2,18},{18,2},{3,19},{19,3},{4,20},{20... | collective-permute-start | bytes 786440 | tf_op jit(solution)/shard_map/ppermute | solution.py:206
  49.1 2.5 %collective-permute-start.9 = (bf16[2,2,128,256]{3,2,1,0:T(8,128)(2,1)S(1)}, bf16[2,2,128,256]{3,2,1,0:T(8,128)(2,1)}, u32[]{:S(2)}, u32[]{:S(2)}) collective-permute-start(bf16[2,2,128,256]{3,2,1,0:T(8,128)(2,1)S(1)} %constant_dynamic-slice_fusion.2), channel_id=1, source_target_pairs={{0,4},{5,1},{4,8},{9,5},{8,12},{13,9},{12,14},{15,13},{14,10},{11,... | collective-permute-start | bytes 786440 | tf_op jit(solution)/shard_map/ppermute | solution.py:232
  51.8 1.6 %collective-permute-start.22 = (bf16[2,2,128,256]{3,2,1,0:T(8,128)(2,1)}, bf16[2,2,128,256]{3,2,1,0:T(8,128)(2,1)}, u32[]{:S(2)}, u32[]{:S(2)}) collective-permute-start(bf16[2,2,128,256]{3,2,1,0:T(8,128)(2,1)} %collective-permute-done.20.refs_1_), channel_id=1, source_target_pairs={{0,4},{5,1},{4,8},{9,5},{8,12},{13,9},{12,14},{15,13},{14,10},{11,... | collective-permute-start | bytes 786440 | tf_op jit(solution)/shard_map/ppermute | solution.py:232
  53.4 2.8 %collective-permute-done.12.refs_11_ = bf16[256,512]{1,0:T(8,128)(2,1)S(1)} collective-permute-done((bf16[256,512]{1,0:T(8,128)(2,1)S(1)}, bf16[256,512]{1,0:T(8,128)(2,1)S(1)}, u32[]{:S(2)}, u32[]{:S(2)}) %collective-permute-start.12) | collective-permute-done | bytes 262176 | tf_op jit(solution)/shard_map/ppermute | solution.py:206
  56.2 0.5 collective-permute-start.10
  56.8 1.7 %collective-permute-done.22.refs_3_ = bf16[2,2,128,256]{3,2,1,0:T(8,128)(2,1)} collective-permute-done((bf16[2,2,128,256]{3,2,1,0:T(8,128)(2,1)}, bf16[2,2,128,256]{3,2,1,0:T(8,128)(2,1)}, u32[]{:S(2)}, u32[]{:S(2)}) %collective-permute-start.22) | collective-permute-done | bytes 262176 | tf_op jit(solution)/shard_map/ppermute | solution.py:232
  58.4 2.4 %collective-permute-start.24 = (bf16[2,2,128,256]{3,2,1,0:T(8,128)(2,1)}, bf16[2,2,128,256]{3,2,1,0:T(8,128)(2,1)S(1)}, u32[]{:S(2)}, u32[]{:S(2)}) collective-permute-start(bf16[2,2,128,256]{3,2,1,0:T(8,128)(2,1)} %collective-permute-done.22.refs_3_), channel_id=1, source_target_pairs={{0,4},{5,1},{4,8},{9,5},{8,12},{13,9},{12,14},{15,13},{14,10},{11,... | collective-permute-start | bytes 786440 | tf_op jit(solution)/shard_map/ppermute | solution.py:232
  60.9 1.7 %collective-permute-start.18 = (bf16[2,1,128,256]{3,2,1,0:T(8,128)(2,1)S(1)}, bf16[2,1,128,256]{3,2,1,0:T(8,128)(2,1)S(1)}, u32[]{:S(2)}, u32[]{:S(2)}) collective-permute-start(bf16[2,1,128,256]{3,2,1,0:T(8,128)(2,1)S(1)} %constant_dynamic-slice_fusion.1), channel_id=1, source_target_pairs={{0,4},{5,1},{4,8},{9,5},{8,12},{13,9},{12,14},{15,13},{14,10},{11,... | collective-permute-start | bytes 393224 | tf_op jit(solution)/shard_map/ppermute | solution.py:232
  62.7 0.5 collective-permute-start.15
  63.2 1.0 %copy-done.3 = bf16[2,4,128,256]{3,2,1,0:T(8,128)(2,1)S(1)} copy-done((bf16[2,4,128,256]{3,2,1,0:T(8,128)(2,1)S(1)}, bf16[2,4,128,256]{3,2,1,0:T(8,128)(2,1)}, u32[]{:S(2)}) %copy-start.3) | copy-done | bytes 524312
  64.3 4.0 %shard_map.113 = (f32[4,256,256]{2,1,0:T(8,128)}, bf16[4,256,256]{2,1,0:T(8,128)(2,1)S(1)}) custom-call(bf16[4,128,256]{2,1,0:T(8,128)(2,1)S(1)} %bitcast.39, bf16[2,4,128,256]{3,2,1,0:T(8,128)(2,1)S(1)} %collective-permute-done.1.refs_1_, bf16[2,4,128,256]{3,2,1,0:T(8,128)(2,1)S(1)} %copy-done.3, ...), custom_call_target="tpu_custom_call" | custom-call | tf_op jit(solution)/shard_map/pallas_call | solution.py:80
  68.4 1.6 %collective-permute-start.28 = (bf16[4,256,256]{2,1,0:T(8,128)(2,1)S(1)}, bf16[4,256,256]{2,1,0:T(8,128)(2,1)S(1)}, u32[]{:S(2)}, u32[]{:S(2)}) collective-permute-start(bf16[4,256,256]{2,1,0:T(8,128)(2,1)S(1)} %get-tuple-element.35), channel_id=1, source_target_pairs={{0,16},{16,0},{1,17},{17,1},{2,18},{18,2},{3,19},{19,3},{4,20},{20... | collective-permute-start | bytes 1572872 | tf_op jit(solution)/shard_map/ppermute | solution.py:206
  70.3 0.8 slice.53
  72.0 0.8 slice.52
  72.8 0.8 slice.51
  73.6 1.6 %collective-permute-done.26.refs_7_ = bf16[2,1,128,256]{3,2,1,0:T(8,128)(2,1)S(1)} collective-permute-done((bf16[2,1,128,256]{3,2,1,0:T(8,128)(2,1)S(1)}, bf16[2,1,128,256]{3,2,1,0:T(8,128)(2,1)S(1)}, u32[]{:S(2)}, u32[]{:S(2)}) %collective-permute-start.26) | collective-permute-done | bytes 131104 | tf_op jit(solution)/shard_map/ppermute | solution.py:232
  75.2 0.6 fusion.prev_ref
  75.8 2.2 %shard_map.114 = (bf16[2,256,256]{2,1,0:T(8,128)(2,1)S(1)}, bf16[2,256,256]{2,1,0:T(8,128)(2,1)S(1)}) custom-call(bf16[2,128,256]{2,1,0:T(8,128)(2,1)S(1)} %get-tuple-element.49.refs_0_, bf16[2,2,128,256]{3,2,1,0:T(8,128)(2,1)S(1)} %copy-done.6, bf16[2,2,128,256]{3,2,1,0:T(8,128)(2,1)S(1)} %collective-permute-done.14.refs_2_, ...), custom_call_target="tpu_custom_call" | custom-call | tf_op jit(solution)/shard_map/pallas_call | solution.py:80
  78.0 2.2 %shard_map.115 = (bf16[2,256,256]{2,1,0:T(8,128)(2,1)S(1)}, bf16[2,256,256]{2,1,0:T(8,128)(2,1)S(1)}) custom-call(bf16[2,128,256]{2,1,0:T(8,128)(2,1)S(1)} %get-tuple-element.48.refs_0_, bf16[2,2,128,256]{3,2,1,0:T(8,128)(2,1)} %collective-permute-done.20.refs_1_, bf16[2,2,128,256]{3,2,1,0:T(8,128)(2,1)S(1)} %collective-permute-done.21.refs_2_, ...), custom_call_target="tpu_custom_call" | custom-call | tf_op jit(solution)/shard_map/pallas_call | solution.py:80
  80.3 2.4 %collective-permute-done.28.other_ref = bf16[4,256,256]{2,1,0:T(8,128)(2,1)S(1)} collective-permute-done((bf16[4,256,256]{2,1,0:T(8,128)(2,1)S(1)}, bf16[4,256,256]{2,1,0:T(8,128)(2,1)S(1)}, u32[]{:S(2)}, u32[]{:S(2)}) %collective-permute-start.28) | collective-permute-done | bytes 524320 | tf_op jit(solution)/shard_map/ppermute | solution.py:206
  82.7 1.7 %shard_map.116 = (f32[8,256,256]{2,1,0:T(8,128)}, bf16[10,256,256]{2,1,0:T(8,128)(2,1)S(1)}) custom-call(s32[1]{0:T(128)} %bitcast.group_ref, f32[4,256,256]{2,1,0:T(8,128)S(1)} %copy-done.1, bf16[4,256,256]{2,1,0:T(8,128)(2,1)S(1)} %collective-permute-done.28.other_ref, bf16[10,256,256]{2,1,0:T(8,128)(2,1)S(1)} %fusion.prev_ref, f32[1,256]{1,0:T(1,128)S(1)} %bitcast.40), custom_call_target="tpu_custom_call" | custom-call | tf_op jit(solution)/shard_map/pallas_call | solution.py:115
  84.5 0.5 collective-permute-start.30
  85.0 1.5 %collective-permute-start.31 = (bf16[2,256,256]{2,1,0:T(8,128)(2,1)S(1)}, bf16[2,256,256]{2,1,0:T(8,128)(2,1)S(1)}, u32[]{:S(2)}, u32[]{:S(2)}) collective-permute-start(bf16[2,256,256]{2,1,0:T(8,128)(2,1)S(1)} %get-tuple-element.32), channel_id=1, source_target_pairs={{0,16},{16,0},{1,17},{17,1},{2,18},{18,2},{3,19},{19,3},{4,20},{20... | collective-permute-start | bytes 786440 | tf_op jit(solution)/shard_map/ppermute | solution.py:206
  86.5 0.5 collective-permute-start.32
  87.0 1.1 %collective-permute-done.30.res_theirs_ref = bf16[3,256,256]{2,1,0:T(8,128)(2,1)S(1)} collective-permute-done((bf16[3,256,256]{2,1,0:T(8,128)(2,1)S(1)}, bf16[3,256,256]{2,1,0:T(8,128)(2,1)S(1)}, u32[]{:S(2)}, u32[]{:S(2)}) %collective-permute-start.30) | collective-permute-done | bytes 393248 | tf_op jit(solution)/shard_map/ppermute | solution.py:206
  88.1 1.6 %copy-done = f32[8,256,256]{2,1,0:T(8,128)S(1)} copy-done((f32[8,256,256]{2,1,0:T(8,128)S(1)}, f32[8,256,256]{2,1,0:T(8,128)}, u32[]{:S(2)}) %copy-start) | copy-done | bytes 2097176
  89.7 4.4 %shard_map.117 = bf16[2048,256]{1,0:T(8,128)(2,1)} custom-call(f32[8,256,256]{2,1,0:T(8,128)S(1)} %copy-done, bf16[10,256,256]{2,1,0:T(8,128)(2,1)S(1)} %get-tuple-element.37.mine_ref, bf16[10,256,256]{2,1,0:T(8,128)(2,1)S(1)} %collective-permute-done.29.theirs_ref, bf16[3,256,256]{2,1,0:T(8,128)(2,1)S(1)} %copy-done.4, ...), custom_call_target="tpu_custom_call" | custom-call | tf_op jit(solution)/shard_map/pallas_call | solution.py:156
  94.2 4.7 %collective-permute-done.32.refs_2_ = bf16[2,256,256]{2,1,0:T(8,128)(2,1)S(1)} collective-permute-done((bf16[2,256,256]{2,1,0:T(8,128)(2,1)S(1)}, bf16[2,256,256]{2,1,0:T(8,128)(2,1)S(1)}, u32[]{:S(2)}, u32[]{:S(2)}) %collective-permute-start.32) | collective-permute-done | bytes 262176 | tf_op jit(solution)/shard_map/ppermute | solution.py:206
  98.8 2.0 %shard_map.118 = bf16[2048,256]{1,0:T(8,128)(2,1)} custom-call(s32[1]{0:T(128)} %bitcast.group_ref, bf16[2,256,256]{2,1,0:T(8,128)(2,1)S(1)} %get-tuple-element.39.refs_0_, bf16[2,256,256]{2,1,0:T(8,128)(2,1)S(1)} %get-tuple-element.40.refs_1_, bf16[2,256,256]{2,1,0:T(8,128)(2,1)S(1)} %collective-permute-done.32.refs_2_, ...), custom_call_target="tpu_custom_call" | custom-call | tf_op jit(solution)/shard_map/pallas_call | solution.py:194
  (84 shorter events, 2.5 us)
Async XLA Ops:
  2.2 5.2 %copy-start.14 = (s32[8]{0:T(128)S(1)}, s32[8]{0:T(128)}, u32[]{:S(2)}) copy-start(s32[8]{0:T(128)} %param.15) | copy-start | bytes 100
  2.2 5.3 %copy-start.11 = (bf16[256,512]{1,0:T(8,128)(2,1)S(1)}, bf16[256,512]{1,0:T(8,128)(2,1)}, u32[]{:S(2)}) copy-start(bf16[256,512]{1,0:T(8,128)(2,1)} %param.10) | copy-start | bytes 786436
  2.2 5.3 %copy-start.12 = (bf16[8,8,256]{2,1,0:T(8,128)(2,1)S(1)}, bf16[8,8,256]{2,1,0:T(8,128)(2,1)}, u32[]{:S(2)}) copy-start(bf16[8,8,256]{2,1,0:T(8,128)(2,1)} %param.13) | copy-start | bytes 98308
  2.2 5.3 %copy-start.13 = (bf16[8,2,256]{2,1,0:T(2,128)(2,1)S(1)}, bf16[8,2,256]{2,1,0:T(2,128)(2,1)}, u32[]{:S(2)}) copy-start(bf16[8,2,256]{2,1,0:T(2,128)(2,1)} %param.14) | copy-start | bytes 24580
  2.3 2.1 %collective-permute-start = (bf16[8,128,256]{2,1,0:T(8,128)(2,1)S(1)}, bf16[8,128,256]{2,1,0:T(8,128)(2,1)S(1)}, u32[]{:S(2)}, u32[]{:S(2)}) collective-permute-start(bf16[8,128,256]{2,1,0:T(8,128)(2,1)S(1)} %pad_maximum_fusion), channel_id=1, source_target_pairs={{0,1},{1,0},{2,3},{3,2},{4,5},{5,4},{6,7},{7,6},{8,9},{9,8},{10,11... | collective-permute-start | bytes 1572872 | tf_op jit(solution)/shard_map/ppermute | solution.py:206
  4.4 10.1 %collective-permute-start.1 = (bf16[2,4,128,256]{3,2,1,0:T(8,128)(2,1)S(1)}, bf16[2,4,128,256]{3,2,1,0:T(8,128)(2,1)S(1)}, u32[]{:S(2)}, u32[]{:S(2)}) collective-permute-start(bf16[2,4,128,256]{3,2,1,0:T(8,128)(2,1)S(1)} %pad_maximum_fusion.1), channel_id=1, source_target_pairs={{0,4},{5,1},{4,8},{9,5},{8,12},{13,9},{12,14},{15,13},{14,10},{11,... | collective-permute-start | bytes 1572872 | tf_op jit(solution)/shard_map/ppermute | solution.py:232
  14.5 20.2 %collective-permute-start.3 = (bf16[2,4,128,256]{3,2,1,0:T(8,128)(2,1)S(1)}, bf16[2,4,128,256]{3,2,1,0:T(8,128)(2,1)S(1)}, u32[]{:S(2)}, u32[]{:S(2)}) collective-permute-start(bf16[2,4,128,256]{3,2,1,0:T(8,128)(2,1)S(1)} %collective-permute-done.1.refs_1_), channel_id=1, source_target_pairs={{0,4},{5,1},{4,8},{9,5},{8,12},{13,9},{12,14},{15,13},{14,10},{11,... | collective-permute-start | bytes 1572872 | tf_op jit(solution)/shard_map/ppermute | solution.py:232
  17.3 23.9 %all-to-all-start = ((bf16[8,40,512]{2,1,0:T(8,128)(2,1)}), bf16[8,40,512]{2,1,0:T(8,128)(2,1)}, u32[]{:S(2)}, u32[]{:S(2)}) async-start(bf16[8,40,512]{2,1,0:T(8,128)(2,1)} %maximum_maximum_fusion), calls=%async_computation | async-start | bytes 655360 | tf_op jit(solution)/shard_map/all_to_all | solution.py:295
  22.1 9.3 %collective-permute-start.5 = (bf16[2,2,128,256]{3,2,1,0:T(8,128)(2,1)S(1)}, bf16[2,2,128,256]{3,2,1,0:T(8,128)(2,1)S(1)}, u32[]{:S(2)}, u32[]{:S(2)}) collective-permute-start(bf16[2,2,128,256]{3,2,1,0:T(8,128)(2,1)S(1)} %pad_maximum_fusion.2), channel_id=1, source_target_pairs={{0,4},{5,1},{4,8},{9,5},{8,12},{13,9},{12,14},{15,13},{14,10},{11,... | collective-permute-start | bytes 786440 | tf_op jit(solution)/shard_map/ppermute | solution.py:232
  31.4 10.8 %copy-start.5 = (bf16[2,2,128,256]{3,2,1,0:T(8,128)(2,1)}, bf16[2,2,128,256]{3,2,1,0:T(8,128)(2,1)S(1)}, u32[]{:S(2)}) copy-start(bf16[2,2,128,256]{3,2,1,0:T(8,128)(2,1)S(1)} %collective-permute-done.5.refs_1_) | copy-start | bytes 786436
  31.4 7.2 %collective-permute-start.8 = (bf16[2,2,128,256]{3,2,1,0:T(8,128)(2,1)S(1)}, bf16[2,2,128,256]{3,2,1,0:T(8,128)(2,1)}, u32[]{:S(2)}, u32[]{:S(2)}) collective-permute-start(bf16[2,2,128,256]{3,2,1,0:T(8,128)(2,1)S(1)} %collective-permute-done.5.refs_1_), channel_id=1, source_target_pairs={{0,4},{5,1},{4,8},{9,5},{8,12},{13,9},{12,14},{15,13},{14,10},{11,... | collective-permute-start | bytes 786440 | tf_op jit(solution)/shard_map/ppermute | solution.py:232
  34.7 9.5 %collective-permute-start.6 = (bf16[2,4,128,256]{3,2,1,0:T(8,128)(2,1)S(1)}, bf16[2,4,128,256]{3,2,1,0:T(8,128)(2,1)S(1)}, u32[]{:S(2)}, u32[]{:S(2)}) collective-permute-start(bf16[2,4,128,256]{3,2,1,0:T(8,128)(2,1)S(1)} %collective-permute-done.3.refs_3_), channel_id=1, source_target_pairs={{0,4},{5,1},{4,8},{9,5},{8,12},{13,9},{12,14},{15,13},{14,10},{11,... | collective-permute-start | bytes 1572872 | tf_op jit(solution)/shard_map/ppermute | solution.py:232
  37.2 9.5 %collective-permute-start.2 = (bf16[2,4,128,256]{3,2,1,0:T(8,128)(2,1)S(1)}, bf16[2,4,128,256]{3,2,1,0:T(8,128)(2,1)S(1)}, u32[]{:S(2)}, u32[]{:S(2)}) collective-permute-start(bf16[2,4,128,256]{3,2,1,0:T(8,128)(2,1)S(1)} %collective-permute-done.1.refs_1_), channel_id=1, source_target_pairs={{0,1},{1,0},{2,3},{3,2},{4,5},{5,4},{6,7},{7,6},{8,9},{9,8},{10,11... | collective-permute-start | bytes 1572872 | tf_op jit(solution)/shard_map/ppermute | solution.py:206
  38.6 10.4 %collective-permute-start.16 = (bf16[2,2,128,256]{3,2,1,0:T(8,128)(2,1)}, bf16[2,2,128,256]{3,2,1,0:T(8,128)(2,1)S(1)}, u32[]{:S(2)}, u32[]{:S(2)}) collective-permute-start(bf16[2,2,128,256]{3,2,1,0:T(8,128)(2,1)} %collective-permute-done.8.refs_3_), channel_id=1, source_target_pairs={{0,4},{5,1},{4,8},{9,5},{8,12},{13,9},{12,14},{15,13},{14,10},{11,... | collective-permute-start | bytes 786440 | tf_op jit(solution)/shard_map/ppermute | solution.py:232
  42.3 9.3 %collective-permute-start.11 = (bf16[256,512]{1,0:T(8,128)(2,1)S(1)}, bf16[256,512]{1,0:T(8,128)(2,1)S(1)}, u32[]{:S(2)}, u32[]{:S(2)}) collective-permute-start(bf16[256,512]{1,0:T(8,128)(2,1)S(1)} %fusion.3.refs_9_), channel_id=1, source_target_pairs={{0,1},{1,0},{2,3},{3,2},{4,5},{5,4},{6,7},{7,6},{8,9},{9,8},{10,11... | collective-permute-start | bytes 786440 | tf_op jit(solution)/shard_map/ppermute | solution.py:206
  44.2 7.5 %collective-permute-start.20 = (bf16[2,2,128,256]{3,2,1,0:T(8,128)(2,1)}, bf16[2,2,128,256]{3,2,1,0:T(8,128)(2,1)}, u32[]{:S(2)}, u32[]{:S(2)}) collective-permute-start(bf16[2,2,128,256]{3,2,1,0:T(8,128)(2,1)} %pad_maximum_fusion.3), channel_id=1, source_target_pairs={{0,4},{5,1},{4,8},{9,5},{8,12},{13,9},{12,14},{15,13},{14,10},{11,... | collective-permute-start | bytes 786440 | tf_op jit(solution)/shard_map/ppermute | solution.py:232
  46.7 14.2 %collective-permute-start.4 = (bf16[2,4,128,256]{3,2,1,0:T(8,128)(2,1)S(1)}, bf16[2,4,128,256]{3,2,1,0:T(8,128)(2,1)}, u32[]{:S(2)}, u32[]{:S(2)}) collective-permute-start(bf16[2,4,128,256]{3,2,1,0:T(8,128)(2,1)S(1)} %collective-permute-done.3.refs_3_), channel_id=1, source_target_pairs={{0,1},{1,0},{2,3},{3,2},{4,5},{5,4},{6,7},{7,6},{8,9},{9,8},{10,11... | collective-permute-start | bytes 1572872 | tf_op jit(solution)/shard_map/ppermute | solution.py:206
  47.5 8.7 %collective-permute-start.12 = (bf16[256,512]{1,0:T(8,128)(2,1)S(1)}, bf16[256,512]{1,0:T(8,128)(2,1)S(1)}, u32[]{:S(2)}, u32[]{:S(2)}) collective-permute-start(bf16[256,512]{1,0:T(8,128)(2,1)S(1)} %fusion.3.refs_9_), channel_id=1, source_target_pairs={{0,16},{16,0},{1,17},{17,1},{2,18},{18,2},{3,19},{19,3},{4,20},{20... | collective-permute-start | bytes 786440 | tf_op jit(solution)/shard_map/ppermute | solution.py:206
  49.1 7.2 %collective-permute-start.9 = (bf16[2,2,128,256]{3,2,1,0:T(8,128)(2,1)S(1)}, bf16[2,2,128,256]{3,2,1,0:T(8,128)(2,1)}, u32[]{:S(2)}, u32[]{:S(2)}) collective-permute-start(bf16[2,2,128,256]{3,2,1,0:T(8,128)(2,1)S(1)} %constant_dynamic-slice_fusion.2), channel_id=1, source_target_pairs={{0,4},{5,1},{4,8},{9,5},{8,12},{13,9},{12,14},{15,13},{14,10},{11,... | collective-permute-start | bytes 786440 | tf_op jit(solution)/shard_map/ppermute | solution.py:232
  51.6 11.6 %collective-permute-start.7 = (bf16[2,4,128,256]{3,2,1,0:T(8,128)(2,1)S(1)}, bf16[2,4,128,256]{3,2,1,0:T(8,128)(2,1)}, u32[]{:S(2)}, u32[]{:S(2)}) collective-permute-start(bf16[2,4,128,256]{3,2,1,0:T(8,128)(2,1)S(1)} %collective-permute-done.6.refs_5_), channel_id=1, source_target_pairs={{0,1},{1,0},{2,3},{3,2},{4,5},{5,4},{6,7},{7,6},{8,9},{9,8},{10,11... | collective-permute-start | bytes 1572872 | tf_op jit(solution)/shard_map/ppermute | solution.py:206
  51.8 6.7 %collective-permute-start.22 = (bf16[2,2,128,256]{3,2,1,0:T(8,128)(2,1)}, bf16[2,2,128,256]{3,2,1,0:T(8,128)(2,1)}, u32[]{:S(2)}, u32[]{:S(2)}) collective-permute-start(bf16[2,2,128,256]{3,2,1,0:T(8,128)(2,1)} %collective-permute-done.20.refs_1_), channel_id=1, source_target_pairs={{0,4},{5,1},{4,8},{9,5},{8,12},{13,9},{12,14},{15,13},{14,10},{11,... | collective-permute-start | bytes 786440 | tf_op jit(solution)/shard_map/ppermute | solution.py:232
  56.2 6.4 %collective-permute-start.13 = (bf16[256,512]{1,0:T(8,128)(2,1)S(1)}, bf16[256,512]{1,0:T(8,128)(2,1)S(1)}, u32[]{:S(2)}, u32[]{:S(2)}) collective-permute-start(bf16[256,512]{1,0:T(8,128)(2,1)S(1)} %collective-permute-done.12.refs_11_), channel_id=1, source_target_pairs={{0,1},{1,0},{2,3},{3,2},{4,5},{5,4},{6,7},{7,6},{8,9},{9,8},{10,11... | collective-permute-start | bytes 786440 | tf_op jit(solution)/shard_map/ppermute | solution.py:206
  56.2 6.4 %collective-permute-start.10 = (bf16[2,2,128,256]{3,2,1,0:T(8,128)(2,1)}, bf16[2,2,128,256]{3,2,1,0:T(8,128)(2,1)}, u32[]{:S(2)}, u32[]{:S(2)}) collective-permute-start(bf16[2,2,128,256]{3,2,1,0:T(8,128)(2,1)} %collective-permute-done.9.refs_7_), channel_id=1, source_target_pairs={{0,1},{1,0},{2,3},{3,2},{4,5},{5,4},{6,7},{7,6},{8,9},{9,8},{10,11... | collective-permute-start | bytes 786440 | tf_op jit(solution)/shard_map/ppermute | solution.py:206
  58.4 11.5 %collective-permute-start.24 = (bf16[2,2,128,256]{3,2,1,0:T(8,128)(2,1)}, bf16[2,2,128,256]{3,2,1,0:T(8,128)(2,1)S(1)}, u32[]{:S(2)}, u32[]{:S(2)}) collective-permute-start(bf16[2,2,128,256]{3,2,1,0:T(8,128)(2,1)} %collective-permute-done.22.refs_3_), channel_id=1, source_target_pairs={{0,4},{5,1},{4,8},{9,5},{8,12},{13,9},{12,14},{15,13},{14,10},{11,... | collective-permute-start | bytes 786440 | tf_op jit(solution)/shard_map/ppermute | solution.py:232
  60.9 7.4 %collective-permute-start.18 = (bf16[2,1,128,256]{3,2,1,0:T(8,128)(2,1)S(1)}, bf16[2,1,128,256]{3,2,1,0:T(8,128)(2,1)S(1)}, u32[]{:S(2)}, u32[]{:S(2)}) collective-permute-start(bf16[2,1,128,256]{3,2,1,0:T(8,128)(2,1)S(1)} %constant_dynamic-slice_fusion.1), channel_id=1, source_target_pairs={{0,4},{5,1},{4,8},{9,5},{8,12},{13,9},{12,14},{15,13},{14,10},{11,... | collective-permute-start | bytes 393224 | tf_op jit(solution)/shard_map/ppermute | solution.py:232
  62.7 7.5 %collective-permute-start.14 = (bf16[2,2,128,256]{3,2,1,0:T(8,128)(2,1)}, bf16[2,2,128,256]{3,2,1,0:T(8,128)(2,1)S(1)}, u32[]{:S(2)}, u32[]{:S(2)}) collective-permute-start(bf16[2,2,128,256]{3,2,1,0:T(8,128)(2,1)} %copy-done.5), channel_id=1, source_target_pairs={{0,1},{1,0},{2,3},{3,2},{4,5},{5,4},{6,7},{7,6},{8,9},{9,8},{10,11... | collective-permute-start | bytes 786440 | tf_op jit(solution)/shard_map/ppermute | solution.py:206
  62.7 8.4 %collective-permute-start.15 = (bf16[2,2,128,256]{3,2,1,0:T(8,128)(2,1)}, bf16[2,2,128,256]{3,2,1,0:T(8,128)(2,1)S(1)}, u32[]{:S(2)}, u32[]{:S(2)}) collective-permute-start(bf16[2,2,128,256]{3,2,1,0:T(8,128)(2,1)} %collective-permute-done.8.refs_3_), channel_id=1, source_target_pairs={{0,1},{1,0},{2,3},{3,2},{4,5},{5,4},{6,7},{7,6},{8,9},{9,8},{10,11... | collective-permute-start | bytes 786440 | tf_op jit(solution)/shard_map/ppermute | solution.py:206
  63.2 8.2 %collective-permute-start.17 = (bf16[2,2,128,256]{3,2,1,0:T(8,128)(2,1)S(1)}, bf16[2,2,128,256]{3,2,1,0:T(8,128)(2,1)S(1)}, u32[]{:S(2)}, u32[]{:S(2)}) collective-permute-start(bf16[2,2,128,256]{3,2,1,0:T(8,128)(2,1)S(1)} %collective-permute-done.16.refs_5_), channel_id=1, source_target_pairs={{0,1},{1,0},{2,3},{3,2},{4,5},{5,4},{6,7},{7,6},{8,9},{9,8},{10,11... | collective-permute-start | bytes 786440 | tf_op jit(solution)/shard_map/ppermute | solution.py:206
  63.2 1.0 %copy-start.3 = (bf16[2,4,128,256]{3,2,1,0:T(8,128)(2,1)S(1)}, bf16[2,4,128,256]{3,2,1,0:T(8,128)(2,1)}, u32[]{:S(2)}) copy-start(bf16[2,4,128,256]{3,2,1,0:T(8,128)(2,1)} %copy-done.2) | copy-start | bytes 1572868
  68.3 7.4 %copy-start.6 = (bf16[2,2,128,256]{3,2,1,0:T(8,128)(2,1)S(1)}, bf16[2,2,128,256]{3,2,1,0:T(8,128)(2,1)}, u32[]{:S(2)}) copy-start(bf16[2,2,128,256]{3,2,1,0:T(8,128)(2,1)} %copy-done.5) | copy-start | bytes 786436
  68.4 14.3 %collective-permute-start.28 = (bf16[4,256,256]{2,1,0:T(8,128)(2,1)S(1)}, bf16[4,256,256]{2,1,0:T(8,128)(2,1)S(1)}, u32[]{:S(2)}, u32[]{:S(2)}) collective-permute-start(bf16[4,256,256]{2,1,0:T(8,128)(2,1)S(1)} %get-tuple-element.35), channel_id=1, source_target_pairs={{0,16},{16,0},{1,17},{17,1},{2,18},{18,2},{3,19},{19,3},{4,20},{20... | collective-permute-start | bytes 1572872 | tf_op jit(solution)/shard_map/ppermute | solution.py:206
  69.9 1.7 %collective-permute-start.19 = (bf16[2,1,128,256]{3,2,1,0:T(8,128)(2,1)S(1)}, bf16[2,1,128,256]{3,2,1,0:T(8,128)(2,1)S(1)}, u32[]{:S(2)}, u32[]{:S(2)}) collective-permute-start(bf16[2,1,128,256]{3,2,1,0:T(8,128)(2,1)S(1)} %collective-permute-done.18.refs_7_), channel_id=1, source_target_pairs={{0,1},{1,0},{2,3},{3,2},{4,5},{5,4},{6,7},{7,6},{8,9},{9,8},{10,11... | collective-permute-start | bytes 393224 | tf_op jit(solution)/shard_map/ppermute | solution.py:206
  70.1 5.0 %collective-permute-start.26 = (bf16[2,1,128,256]{3,2,1,0:T(8,128)(2,1)S(1)}, bf16[2,1,128,256]{3,2,1,0:T(8,128)(2,1)S(1)}, u32[]{:S(2)}, u32[]{:S(2)}) collective-permute-start(bf16[2,1,128,256]{3,2,1,0:T(8,128)(2,1)S(1)} %constant_dynamic-slice_fusion), channel_id=1, source_target_pairs={{0,4},{5,1},{4,8},{9,5},{8,12},{13,9},{12,14},{15,13},{14,10},{11,... | collective-permute-start | bytes 393224 | tf_op jit(solution)/shard_map/ppermute | solution.py:232
  71.1 6.9 %collective-permute-start.21 = (bf16[2,2,128,256]{3,2,1,0:T(8,128)(2,1)}, bf16[2,2,128,256]{3,2,1,0:T(8,128)(2,1)S(1)}, u32[]{:S(2)}, u32[]{:S(2)}) collective-permute-start(bf16[2,2,128,256]{3,2,1,0:T(8,128)(2,1)} %collective-permute-done.20.refs_1_), channel_id=1, source_target_pairs={{0,1},{1,0},{2,3},{3,2},{4,5},{5,4},{6,7},{7,6},{8,9},{9,8},{10,11... | collective-permute-start | bytes 786440 | tf_op jit(solution)/shard_map/ppermute | solution.py:206
  71.4 6.6 %collective-permute-start.23 = (bf16[2,2,128,256]{3,2,1,0:T(8,128)(2,1)}, bf16[2,2,128,256]{3,2,1,0:T(8,128)(2,1)S(1)}, u32[]{:S(2)}, u32[]{:S(2)}) collective-permute-start(bf16[2,2,128,256]{3,2,1,0:T(8,128)(2,1)} %collective-permute-done.22.refs_3_), channel_id=1, source_target_pairs={{0,1},{1,0},{2,3},{3,2},{4,5},{5,4},{6,7},{7,6},{8,9},{9,8},{10,11... | collective-permute-start | bytes 786440 | tf_op jit(solution)/shard_map/ppermute | solution.py:206
  71.7 6.3 %collective-permute-start.25 = (bf16[2,2,128,256]{3,2,1,0:T(8,128)(2,1)S(1)}, bf16[2,2,128,256]{3,2,1,0:T(8,128)(2,1)S(1)}, u32[]{:S(2)}, u32[]{:S(2)}) collective-permute-start(bf16[2,2,128,256]{3,2,1,0:T(8,128)(2,1)S(1)} %collective-permute-done.24.refs_5_), channel_id=1, source_target_pairs={{0,1},{1,0},{2,3},{3,2},{4,5},{5,4},{6,7},{7,6},{8,9},{9,8},{10,11... | collective-permute-start | bytes 786440 | tf_op jit(solution)/shard_map/ppermute | solution.py:206
  75.2 2.9 %collective-permute-start.27 = (bf16[2,1,128,256]{3,2,1,0:T(8,128)(2,1)S(1)}, bf16[2,1,128,256]{3,2,1,0:T(8,128)(2,1)S(1)}, u32[]{:S(2)}, u32[]{:S(2)}) collective-permute-start(bf16[2,1,128,256]{3,2,1,0:T(8,128)(2,1)S(1)} %collective-permute-done.26.refs_7_), channel_id=1, source_target_pairs={{0,1},{1,0},{2,3},{3,2},{4,5},{5,4},{6,7},{7,6},{8,9},{9,8},{10,11... | collective-permute-start | bytes 393224 | tf_op jit(solution)/shard_map/ppermute | solution.py:206
  78.0 4.7 %copy-start.1 = (f32[4,256,256]{2,1,0:T(8,128)S(1)}, f32[4,256,256]{2,1,0:T(8,128)}, u32[]{:S(2)}) copy-start(f32[4,256,256]{2,1,0:T(8,128)} %get-tuple-element.33.own_ref) | copy-start | bytes 3145732
  78.0 4.7 %copy-start.8 = (f32[256]{0:T(256)S(1)}, f32[256]{0:T(256)}, u32[]{:S(2)}) copy-start(f32[256]{0:T(256)} %param.12) | copy-start | bytes 3076
  82.7 1.8 %copy-start.4 = (bf16[3,256,256]{2,1,0:T(8,128)(2,1)S(1)}, bf16[3,256,256]{2,1,0:T(8,128)(2,1)}, u32[]{:S(2)}) copy-start(bf16[3,256,256]{2,1,0:T(8,128)(2,1)} %res_mine_ref.1) | copy-start | bytes 1179652
  82.7 5.4 %copy-start.7 = (bf16[256,256]{1,0:T(8,128)(2,1)S(1)}, bf16[256,256]{1,0:T(8,128)(2,1)}, u32[]{:S(2)}) copy-start(bf16[256,256]{1,0:T(8,128)(2,1)} %skip_ref.1) | copy-start | bytes 393220
  82.7 5.4 %copy-start.9 = (f32[256]{0:T(256)S(1)}, f32[256]{0:T(256)}, u32[]{:S(2)}) copy-start(f32[256]{0:T(256)} %param.17) | copy-start | bytes 3076
  82.7 5.4 %copy-start.10 = (f32[256]{0:T(256)S(1)}, f32[256]{0:T(256)}, u32[]{:S(2)}) copy-start(f32[256]{0:T(256)} %param.19) | copy-start | bytes 3076
  84.5 3.6 %collective-permute-start.29 = (bf16[10,256,256]{2,1,0:T(8,128)(2,1)S(1)}, bf16[10,256,256]{2,1,0:T(8,128)(2,1)S(1)}, u32[]{:S(2)}, u32[]{:S(2)}) collective-permute-start(bf16[10,256,256]{2,1,0:T(8,128)(2,1)S(1)} %get-tuple-element.37.mine_ref), channel_id=1, source_target_pairs={{0,1},{1,0},{2,3},{3,2},{4,5},{5,4},{6,7},{7,6},{8,9},{9,8},{10,11... | collective-permute-start | bytes 3932168 | tf_op jit(solution)/shard_map/ppermute | solution.py:206
  84.5 3.6 %collective-permute-start.30 = (bf16[3,256,256]{2,1,0:T(8,128)(2,1)S(1)}, bf16[3,256,256]{2,1,0:T(8,128)(2,1)S(1)}, u32[]{:S(2)}, u32[]{:S(2)}) collective-permute-start(bf16[3,256,256]{2,1,0:T(8,128)(2,1)S(1)} %copy-done.4), channel_id=1, source_target_pairs={{0,1},{1,0},{2,3},{3,2},{4,5},{5,4},{6,7},{7,6},{8,9},{9,8},{10,11... | collective-permute-start | bytes 1179656 | tf_op jit(solution)/shard_map/ppermute | solution.py:206
  85.0 9.2 %collective-permute-start.31 = (bf16[2,256,256]{2,1,0:T(8,128)(2,1)S(1)}, bf16[2,256,256]{2,1,0:T(8,128)(2,1)S(1)}, u32[]{:S(2)}, u32[]{:S(2)}) collective-permute-start(bf16[2,256,256]{2,1,0:T(8,128)(2,1)S(1)} %get-tuple-element.32), channel_id=1, source_target_pairs={{0,16},{16,0},{1,17},{17,1},{2,18},{18,2},{3,19},{19,3},{4,20},{20... | collective-permute-start | bytes 786440 | tf_op jit(solution)/shard_map/ppermute | solution.py:206
  86.5 12.3 %collective-permute-start.32 = (bf16[2,256,256]{2,1,0:T(8,128)(2,1)S(1)}, bf16[2,256,256]{2,1,0:T(8,128)(2,1)S(1)}, u32[]{:S(2)}, u32[]{:S(2)}) collective-permute-start(bf16[2,256,256]{2,1,0:T(8,128)(2,1)S(1)} %get-tuple-element.29), channel_id=1, source_target_pairs={{0,16},{16,0},{1,17},{17,1},{2,18},{18,2},{3,19},{19,3},{4,20},{20... | collective-permute-start | bytes 786440 | tf_op jit(solution)/shard_map/ppermute | solution.py:206
  88.1 1.6 %copy-start = (f32[8,256,256]{2,1,0:T(8,128)S(1)}, f32[8,256,256]{2,1,0:T(8,128)}, u32[]{:S(2)}) copy-start(f32[8,256,256]{2,1,0:T(8,128)} %get-tuple-element.36.up_ref) | copy-start | bytes 6291460
  (1 other events, 0.8 us)
